TPU v7x, 32 devices: a whole 2x2x4 slice. The times are simulated.
32 devices in a mesh: groups: 2 (over x), rows: 16 (over z, y, core).
Axes of the slice: x: 2, y: 2, z: 4, core: 2. Of those that a mesh axis runs over, the one named last changes fastest.
Arguments:
- sequence_features: bfloat16 [2048, 32, 64], P(('groups', 'rows')), parts along dimension 0
- sequence_presence: int32 [2048, 32], P(('groups', 'rows')), parts along dimension 0, may hold values from 0 to 1, as said below
- position_presence: int32 [64], P('groups'), parts along dimension 0, may hold values from 0 to 1, as said below
- product_scale_vector: float32 [64], replicated, may hold values from 0.1 to 1.9
- product_shift_vector: float32 [64], replicated, may hold values from -3 to 3
- first_factor_matrix: bfloat16 [64, 32], replicated, may hold values from -0.75 to 0.75
- second_factor_matrix: bfloat16 [64, 32], replicated, may hold values from -0.75 to 0.75
- coupling_matrix: bfloat16 [1024, 128], replicated, may hold values from -0.1875 to 0.1875
- coupling_offset: float32 [128], replicated, may hold values from -3 to 3
- feedforward_scale_vector: float32 [64], replicated, may hold values from 0.1 to 1.9
- feedforward_shift_vector: float32 [64], replicated, may hold values from -3 to 3
- feedforward_switch_matrix: bfloat16 [64, 256], replicated, may hold values from -0.75 to 0.75
- feedforward_expand_matrix: bfloat16 [64, 256], replicated, may hold values from -0.75 to 0.75
- feedforward_contract_matrix: bfloat16 [256, 64], replicated, may hold values from -0.375 to 0.375
Outputs:
- pair_mean_update: float32 [2048, 128], P(('groups', 'rows')), parts along dimension 0
- refreshed_sequences: bfloat16 [2048, 32, 64], P(('groups', 'rows')), parts along dimension 0
There are 2 independent parts, one for each index of `groups`. A program takes and returns all parts, laid end to end along the dimension named above; an argument that names none is the same for every part. Nothing has to cross between parts.
Inputs may be any that keep to these rules, and one draw needn't show every extreme that they name: `sequence_presence`: 0 or 1; rows further down the MSA are less often valid. `position_presence`: 0 or 1; the last residue is invalid.
All inputs are finite; a program needn't handle non-finite values.
Results may differ from a plain program's by a relative error of at most 0.0046.
Values sent between devices are 32-bit elements; how exact they have to be, the bound alone decides.
No kernel may reach another device: no remote copies, remote signals or barrier semaphores. Data moves between devices by JAX's collectives and lax.ppermute only.
A program may use at most 128 MiB of HBM per device.

v0:
```python
import jax
import jax.numpy as jnp
from jax import lax
from jax.sharding import PartitionSpec as P


def standardize_features(values, gain, bias):
    values = values.astype(jnp.float32)
    mean = jnp.mean(values, axis=-1, keepdims=True)
    centered = values - mean
    variance = jnp.mean(centered * centered, axis=-1, keepdims=True)
    return centered / jnp.sqrt(variance + 1e-05) * gain + bias


def body(
    sequence_features,
    sequence_presence,
    position_presence,
    product_scale_vector,
    product_shift_vector,
    first_factor_matrix,
    second_factor_matrix,
    coupling_matrix,
    coupling_offset,
    feedforward_scale_vector,
    feedforward_shift_vector,
    feedforward_switch_matrix,
    feedforward_expand_matrix,
    feedforward_contract_matrix,
):
    position_total = sequence_features.shape[1]
    hidden = first_factor_matrix.shape[1]
    valid_flags = (sequence_presence * position_presence[None, :]).astype(jnp.float32)
    standardized_lines = standardize_features(
        sequence_features, product_scale_vector, product_shift_vector
    ).astype(jnp.bfloat16)
    left = (
        jnp.dot(standardized_lines, first_factor_matrix, preferred_element_type=jnp.float32)
        * valid_flags[:, :, None]
    ).astype(jnp.bfloat16)
    right = (
        jnp.dot(standardized_lines, second_factor_matrix, preferred_element_type=jnp.float32)
        * valid_flags[:, :, None]
    ).astype(jnp.bfloat16)
    outer = jnp.einsum("sih,sjk->ijhk", left, right, preferred_element_type=jnp.float32)
    outer = outer.reshape(position_total * position_total, hidden * hidden)
    valid_low = valid_flags.astype(jnp.bfloat16)
    counts = jnp.dot(valid_low.T, valid_low, preferred_element_type=jnp.float32).reshape(
        position_total * position_total
    )
    weight_wide = coupling_matrix.astype(jnp.float32)
    summed, counted = (
        lax.psum_scatter(outer, "rows", scatter_dimension=0, tiled=True),
        lax.psum_scatter(counts, "rows", scatter_dimension=0, tiled=True),
    )
    projected = jnp.dot(summed, weight_wide, precision=lax.Precision.HIGHEST)
    pair_mean_update = projected / jnp.maximum(counted, 1.0)[:, None] + coupling_offset
    feedforward_standardized = standardize_features(
        sequence_features, feedforward_scale_vector, feedforward_shift_vector
    ).astype(jnp.bfloat16)
    gate = jnp.dot(
        feedforward_standardized, feedforward_switch_matrix, preferred_element_type=jnp.float32
    )
    upper = jnp.dot(
        feedforward_standardized, feedforward_expand_matrix, preferred_element_type=jnp.float32
    )
    feedforward_inner = (jax.nn.silu(gate) * upper).astype(jnp.bfloat16)
    refreshed_sequences = (
        sequence_features.astype(jnp.float32)
        + jnp.dot(
            feedforward_inner, feedforward_contract_matrix, preferred_element_type=jnp.float32
        )
    ).astype(jnp.bfloat16)
    return (pair_mean_update, refreshed_sequences)


def solution(mesh):
    in_specs = (
        P(("groups", "rows"), None, None),
        P(("groups", "rows"), None),
        P("groups"),
        P(),
        P(),
        P(),
        P(),
        P(),
        P(),
        P(),
        P(),
        P(),
        P(),
        P(),
    )
    out_specs = (P(("groups", "rows"), None), P(("groups", "rows"), None, None))
    return jax.shard_map(body, mesh=mesh, in_specs=in_specs, out_specs=out_specs, check_vma=False)
```

profile of v0, /device:TPU:0, one launch (start us, length us, event | category | flops | bytes accessed | tf_op | source)
XLA Modules:
  0.0 136.0 jit_solution(1064096451063637105)
XLA Ops:
  7.2 0.0 copy-start
  7.2 0.0 copy-start.2
  7.2 0.0 copy-start.3
  7.2 0.0 reduce-scatter.2.cloned.1.call-start
  7.2 1.4 %convert_reduce_fusion = f32[64,32]{1,0:T(8,128)S(1)} fusion(bf16[64,32,64]{2,1,0:T(8,128)(2,1)} %param.14), kind=kLoop, calls=%fused_computation.4 | loop fusion | flops 260096 | bytes 270336 | tf_op jit(solution)/shard_map/reduce_sum | solution.py:9
  8.7 1.7 %fusion.9 = f32[64,32]{1,0:T(8,128)S(1)} fusion(bf16[64,32,64]{2,1,0:T(8,128)(2,1)} %param.14, f32[64,32]{1,0:T(8,128)S(1)} %broadcast_multiply_fusion), kind=kLoop, calls=%fused_computation.17 | loop fusion | flops 522240 | bytes 278528 | tf_op jit(solution)/shard_map/reduce_sum | solution.py:11
  10.4 0.8 multiply_convert_fusion.1
  11.2 1.7 %add_convert_fusion.1 = bf16[64,32,64]{2,1,0:T(8,128)(2,1)S(1)} fusion(bf16[64,32,64]{2,1,0:T(8,128)(2,1)} %param.14, f32[64]{0:T(128)} %param.18, f32[64]{0:T(128)} %param.17, f32[64,32]{1,0:T(8,128)S(1)} %add_sqrt_fusion, f32[64,32]{1,0:T(8,128)S(1)} %broadcast_multiply_fusion), kind=kLoop, calls=%fused_computation.20 | loop fusion | flops 786432 | bytes 541184 | tf_op jit(solution)/shard_map/convert_element_type | solution.py:36
  12.9 0.0 copy-done.2
  12.9 0.6 fusion.6
  13.5 0.0 copy-done.3
  13.5 7.3 %convolution_bitcast_fusion = f32[32,32,32,32]{2,3,0,1:T(8,128)} fusion(bf16[64,32,32,1]{0,2,1,3:T(8,128)(2,1)S(1)} %fusion.6, bf16[64,32,64]{2,1,0:T(8,128)(2,1)S(1)} %add_convert_fusion.1, f32[64,32]{0,1:T(8,128)S(1)} %multiply_convert_fusion.1, bf16[64,32]{0,1:T(8,128)(2,1)S(1)} %copy-done.3), kind=kOutput, calls=%fused_computation | convolution fusion | flops 142737408 | bytes 4599808 | tf_op jit(solution)/shard_map/sih,sjk->ijhk/dot_general | solution.py:45
  20.8 17.5 %copy.19 = f32[32,32,32,32]{3,2,1,0:T(8,128)} copy(f32[32,32,32,32]{2,3,0,1:T(8,128)} %convolution_bitcast_fusion) | data formatting | bytes 8388608 | tf_op jit(solution)/shard_map/sih,sjk->ijhk/transpose | solution.py:45
  38.3 13.7 %reshape.30 = f32[1024,1024]{1,0:T(8,128)} reshape(f32[32,32,32,32]{3,2,1,0:T(8,128)} %copy.19) | data formatting | bytes 8388608 | tf_op jit(solution)/shard_map/reshape | solution.py:46
  52.0 0.0 copy-start.10
  52.0 0.0 copy-start.1
  52.0 0.0 copy-start.5
  52.0 0.0 copy-start.8
  52.0 0.0 copy-start.9
  52.0 0.0 reduce-scatter.2.cloned.1.call-update
  52.0 0.1 fusion.23
  52.2 0.1 reshape.31
  52.2 0.4 copy-done.10
  52.6 0.6 dynamic-slice
  53.9 35.1 %all-reduce = f32[1024]{0:T(1024)S(1)} all-reduce(f32[1024]{0:T(1024)S(1)} %reshape.31), channel_id=3, replica_groups=mesh['groups'=2,'rows'=16] {'rows'}, use_global_device_ids=true, to_apply=%region_3.0.clone | all-reduce | flops 1024 | bytes 8192
  89.0 0.1 dynamic-slice_maximum_fusion
  89.1 0.0 copy-done.1
  89.1 0.0 copy-done.5
  89.1 0.0 copy-done.8
  89.1 0.0 copy-done.9
  89.1 0.0 copy-start.6
  89.1 0.0 copy-start.7
  89.1 0.7 fusion.16
  89.9 0.0 copy-done.6
  89.9 0.0 copy-done.7
  89.9 0.0 copy-start.4
  89.9 1.8 %fusion.1 = bf16[64,32,64]{2,1,0:T(8,128)(2,1)} fusion(f32[64,32,256]{2,1,0:T(8,128)S(1)} %fusion.16, bf16[64,32,64]{2,1,0:T(8,128)(2,1)S(1)} %copy-done.1, bf16[256,64]{0,1:T(8,128)(2,1)S(1)} %copy-done.6, bf16[64,256]{1,0:T(8,128)(2,1)S(1)} %copy-done.7, f32[64]{0:T(128)S(1)} %copy-done.8, f32[64]{0:T(128)S(1)} %copy-done.9, ...), kind=kOutput, calls=%fused_computation.6 | convolution fusion | flops 138543104 | bytes 2703872 | tf_op jit(solution)/shard_map/dot_general | solution.py:70
  91.7 35.6 %reduce-scatter.2.cloned.1.call-done = f32[64,1024]{1,0:T(8,128)} async-done(((f32[1024,1024]{1,0:T(8,128)}), f32[64,1024]{1,0:T(8,128)}) %reduce-scatter.2.cloned.1.call-update) | async-done | bytes 262160 | tf_op jit(solution)/shard_map/reduce_scatter | solution.py:53
  127.3 0.0 copy-done
  127.3 0.0 copy-done.4
  127.3 1.8 %fusion.8 = f32[64,128]{1,0:T(8,128)} fusion(f32[64,1024]{1,0:T(8,128)} %reduce-scatter.2.cloned.1.call-done, bf16[1024,128]{1,0:T(8,128)(2,1)S(1)} %copy-done, f32[128]{0:T(128)S(1)} %copy-done.4, f32[64]{0:T(128)S(1)} %dynamic-slice_maximum_fusion), kind=kOutput, calls=%fused_computation.16 | convolution fusion | flops 100679680 | bytes 557824 | tf_op jit(solution)/shard_map/dot_general | solution.py:56
  (2 shorter events, 0.0 us)
Async XLA Ops:
  7.2 120.2 %copy-start = (bf16[1024,128]{1,0:T(8,128)(2,1)S(1)}, bf16[1024,128]{1,0:T(8,128)(2,1)}, u32[]{:S(2)}) copy-start(bf16[1024,128]{1,0:T(8,128)(2,1)} %param.21) | copy-start | bytes 786436
  7.2 5.7 %copy-start.2 = (bf16[64,32]{0,1:T(8,128)(2,1)S(1)}, bf16[64,32]{0,1:T(8,128)(2,1)}, u32[]{:S(2)}) copy-start(bf16[64,32]{0,1:T(8,128)(2,1)} %param.19) | copy-start | bytes 12292
  7.2 6.3 %copy-start.3 = (bf16[64,32]{0,1:T(8,128)(2,1)S(1)}, bf16[64,32]{0,1:T(8,128)(2,1)}, u32[]{:S(2)}) copy-start(bf16[64,32]{0,1:T(8,128)(2,1)} %param.20) | copy-start | bytes 12292
  7.2 120.1 %reduce-scatter.2.cloned.1.call-start = ((), (), s32[]{:S(2)}) async-start(), calls=%async_computation.1 | async-start | bytes 4456448 | tf_op jit(solution)/shard_map/reduce_scatter | solution.py:53
  52.0 0.7 copy-start.10
  52.0 37.1 %copy-start.1 = (bf16[64,32,64]{2,1,0:T(8,128)(2,1)S(1)}, bf16[64,32,64]{2,1,0:T(8,128)(2,1)}, u32[]{:S(2)}) copy-start(bf16[64,32,64]{2,1,0:T(8,128)(2,1)} %param.14) | copy-start | bytes 786436
  52.0 37.1 %copy-start.5 = (bf16[64,256]{1,0:T(8,128)(2,1)S(1)}, bf16[64,256]{1,0:T(8,128)(2,1)}, u32[]{:S(2)}) copy-start(bf16[64,256]{1,0:T(8,128)(2,1)} %param.26) | copy-start | bytes 98308
  52.0 37.1 %copy-start.8 = (f32[64]{0:T(128)S(1)}, f32[64]{0:T(128)}, u32[]{:S(2)}) copy-start(f32[64]{0:T(128)} %param.24) | copy-start | bytes 772
  52.0 37.1 %copy-start.9 = (f32[64]{0:T(128)S(1)}, f32[64]{0:T(128)}, u32[]{:S(2)}) copy-start(f32[64]{0:T(128)} %param.23) | copy-start | bytes 772
  89.1 0.8 copy-start.6
  89.1 0.8 copy-start.7
  89.9 37.4 %copy-start.4 = (f32[128]{0:T(128)S(1)}, f32[128]{0:T(128)}, u32[]{:S(2)}) copy-start(f32[128]{0:T(128)} %param.22) | copy-start | bytes 1540
Sparse Core Ops, SparseCore 0:
  52.2 75.1 reduce-scatter.1
where the time goes:
time: 137 us; the launch traced here: 136 us
  waiting for transfers between devices  35.6 us (26%)
  blocking collectives  35.1 us (26%)
  local copies, waits for them, and re-layouts  32.3 us (24%)
  between operations  14.8 us (11%)
  matrix products  12.5 us (9%)
  other arithmetic  5.66 us (4%)
    reduce_scatter x1, waiting for transfers between devices, body(): lax.psum_scatter(outer, 'rows', scatter_dimension=0, tiled=True)  35.6 us
    unnamed x1, blocking collectives  35.1 us
    transpose x1, local copies, waits for them, and re-layouts, body(): jnp.einsum('sih,sjk->ijhk', left, right, preferred_element_type=jnp.float32)  17.5 us
    reshape x1, local copies, waits for them, and re-layouts, body(): outer = outer.reshape(position_total * position_total, hidden * hidden)  13.7 us
    dot_general x1, matrix products, body(): jnp.einsum('sih,sjk->ijhk', left, right, preferred_element_type=jnp.float32)  7.32 us
  transfers between devices with their start and end apart: 1, of which 1 were waited for; matrix products, arithmetic and copies ran while one was open for 3% of the time, Pallas kernels for 0%

commit v1 on v0

v1 whole, which is shorter than its diff:
```python
import functools

import jax
import jax.numpy as jnp
from jax import lax
from jax.experimental import pallas as pl
from jax.experimental.pallas import tpu as pltpu
from jax.sharding import PartitionSpec as P

F32 = jnp.float32
BF16 = jnp.bfloat16
EPS = 1e-05
LANES = 128


def dot(a, b, dims=((1,), (0,))):
    return lax.dot_general(a, b, (dims, ((), ())), preferred_element_type=F32)


def two_halves(array, half):
    return jnp.concatenate([array[:, :half, :], array[:, half:, :]], axis=-1)


def twice(vector):
    return jnp.concatenate([vector, vector], axis=-1)


def block_pair(matrix):
    zero = jnp.zeros_like(matrix)
    return jnp.concatenate(
        [jnp.concatenate([matrix, zero], axis=1), jnp.concatenate([zero, matrix], axis=1)], axis=0
    )


def mean_matrix(channels):
    row = lax.broadcasted_iota(jnp.int32, (2 * channels, 2 * channels), 0) // channels
    column = lax.broadcasted_iota(jnp.int32, (2 * channels, 2 * channels), 1) // channels
    return jnp.where(row == column, 1.0 / channels, 0.0).astype(BF16)


def standardize_pairs(values, averaging, gain, bias):
    wide = values.astype(F32)
    centered = wide - dot(values, averaging)
    variance = dot((centered * centered).astype(BF16), averaging)
    return centered * lax.rsqrt(variance + EPS) * gain + bias


def outer_kernel(
    x_hbm, presence_hbm, position_hbm, gain_hbm, bias_hbm, first_hbm, second_hbm, coupling_hbm,
    out_ref,
    x_ref, presence_ref, position_ref, gain_ref, bias_ref, first_ref, second_ref, coupling_ref, arrived,
    x_scratch, left_t_scratch, left_scratch, x_mat,
):
    copies = [
        pltpu.make_async_copy(source, target, arrived.at[n])
        for n, (source, target) in enumerate((
            (x_hbm, x_ref),
            (presence_hbm, presence_ref),
            (position_hbm, position_ref),
            (gain_hbm, gain_ref),
            (bias_hbm, bias_ref),
            (first_hbm, first_ref),
            (second_hbm, second_ref),
            (coupling_hbm, coupling_ref),
        ))
    ]
    for copy in copies:
        copy.start()
    rows, residues, channels = x_ref.shape
    hidden = first_ref.shape[0]
    half = residues // 2
    quad = LANES // hidden
    groups = hidden // quad

    for copy in copies[:-1]:
        copy.wait()
    x_scratch[...] = two_halves(x_ref[...], half).astype(F32).reshape(rows * half, 2 * channels)
    tokens = jnp.concatenate(
        [x_scratch[pl.ds(p, rows, stride=half), :] for p in range(half)], axis=0
    ).astype(BF16)
    normed = standardize_pairs(tokens, mean_matrix(channels), twice(gain_ref[...]), twice(bias_ref[...]))

    square = (residues, residues)
    diagonal = lax.broadcasted_iota(jnp.int32, square, 0) == lax.broadcasted_iota(jnp.int32, square, 1)
    position = jnp.where(diagonal, position_ref[...].astype(F32), 0.0).sum(axis=1, keepdims=True)
    valid = (presence_ref[...].astype(F32) * position).astype(BF16)
    spread_row = lax.broadcasted_iota(jnp.int32, (residues, half * 2 * channels), 0)
    spread_column = lax.broadcasted_iota(jnp.int32, (residues, half * 2 * channels), 1)
    wanted = spread_column // (2 * channels) + half * ((spread_column % (2 * channels)) // channels)
    spread = jnp.where(spread_row == wanted, 1.0, 0.0).astype(BF16)
    flags = dot(valid, spread, ((0,), (0,)))
    flags = jnp.concatenate(
        [flags[:, p * 2 * channels : (p + 1) * 2 * channels] for p in range(half)], axis=0
    )
    normed = (normed * flags).astype(BF16)

    left_t = dot(block_pair(first_ref[...]), normed, ((1,), (1,)))
    for v in range(left_t_scratch.shape[0]):
        left_t_scratch[v] = left_t[:, v * LANES : (v + 1) * LANES]
    low = lax.broadcasted_iota(jnp.int32, (groups, LANES), 1) < rows
    per = LANES // rows
    for side in range(2):
        for v in range(half // per):
            pieces = [
                left_t_scratch[v, pl.ds(side * hidden + h4, groups, stride=quad), :]
                for h4 in range(quad)
            ]
            turned = [pltpu.roll(piece, rows, 1) for piece in pieces]
            for odd in range(2):
                residue = side * half + v * per + odd
                for c in range(quad // 2):
                    if odd:
                        tile = jnp.where(low, turned[2 * c], pieces[2 * c + 1])
                    else:
                        tile = jnp.where(low, pieces[2 * c], turned[2 * c + 1])
                    left_scratch[c, pl.ds(residue, groups, stride=residues), :] = tile
    left = jnp.concatenate(
        [left_scratch[c] for c in range(quad // 2)], axis=1
    ).astype(BF16)

    second = second_ref[...]
    repeated = jnp.concatenate([second] * quad, axis=0)
    right = dot(normed, block_pair(repeated), ((1,), (1,))).astype(BF16)
    lane_group = lax.broadcasted_iota(jnp.int32, (rows, LANES), 1) // hidden
    masks = [lane_group == h4 for h4 in range(quad)]
    zero = jnp.zeros((rows, LANES), BF16)
    for j in range(residues):
        side, p = j // half, j % half
        one = right[p * rows : (p + 1) * rows, side * LANES : (side + 1) * LANES]
        spread_right = jnp.concatenate([jnp.where(m, one, zero) for m in masks], axis=0)
        product = dot(left, spread_right).astype(BF16)
        for g in range(groups):
            x_mat[j * residues : (j + 1) * residues, g * LANES : (g + 1) * LANES] = product[
                g * residues : (g + 1) * residues, :
            ]
    copies[-1].wait()
    projected = dot(x_mat[...], coupling_ref[...])
    for j in range(residues - 1):
        out_ref[pl.ds(j, residues, stride=residues), :] = projected[j * residues : (j + 1) * residues, :]
    counts = dot(valid, valid, ((1,), (1,)))
    out_ref[pl.ds(residues - 1, residues, stride=residues), :] = jnp.concatenate(
        [counts, jnp.zeros((residues, LANES - residues), F32)], axis=1
    )


def transition_kernel(x_ref, gain_ref, bias_ref, switch_ref, expand_ref, contract_ref, out_ref):
    rows, residues, channels = x_ref.shape
    half = residues // 2
    averaging = mean_matrix(channels)
    gain, bias = twice(gain_ref[...]), twice(bias_ref[...])
    switch = block_pair(switch_ref[...])
    expand = block_pair(expand_ref[...])
    contract = block_pair(contract_ref[...])
    step = 16
    for start in range(0, rows, step):
        pairs = two_halves(x_ref[start : start + step], half).reshape(step * half, 2 * channels)
        normed = standardize_pairs(pairs, averaging, gain, bias).astype(BF16)
        gate = dot(normed, switch) * 0.5
        inner = ((gate + gate * jnp.tanh(gate)) * dot(normed, expand)).astype(BF16)
        result = (pairs.astype(F32) + dot(inner, contract, ((1,), (1,)))).astype(BF16)
        result = result.reshape(step, half, 2 * channels)
        out_ref[start : start + step, :half, :] = result[:, :, :channels]
        out_ref[start : start + step, half:, :] = result[:, :, channels:]


def pick(array, index, axis):
    return lax.dynamic_index_in_dim(array, index, axis, keepdims=False)


def scatter_sum(partial, size):
    me = lax.axis_index("rows")
    tail = partial.shape[1:]
    done = 1
    while size // done > 4 or (size // done) % 4:
        left = size // done
        parts = partial.reshape((left // 2, 2) + tail)
        mine = (me // done) % 2
        partner = [(i, i ^ done) for i in range(size)]
        partial = pick(parts, mine, 1) + lax.ppermute(pick(parts, 1 - mine, 1), "rows", partner)
        done *= 2
    mine = me // done
    total = pick(partial, mine, 0)
    for k in range(1, size // done):
        partner = [(i, i ^ (k * done)) for i in range(size)]
        total = total + lax.ppermute(pick(partial, mine ^ k, 0), "rows", partner)
    return total


def body(
    sequence_features,
    sequence_presence,
    position_presence,
    product_scale_vector,
    product_shift_vector,
    first_factor_matrix,
    second_factor_matrix,
    coupling_matrix,
    coupling_offset,
    feedforward_scale_vector,
    feedforward_shift_vector,
    feedforward_switch_matrix,
    feedforward_expand_matrix,
    feedforward_contract_matrix,
    *,
    size,
):
    rows, residues, channels = sequence_features.shape
    hidden = first_factor_matrix.shape[1]
    pair_channels = coupling_matrix.shape[1]
    pairs = residues * residues
    row = lambda v: v.reshape(1, -1)
    operands = (
        sequence_features,
        sequence_presence.T,
        row(position_presence),
        row(product_scale_vector),
        row(product_shift_vector),
        first_factor_matrix.T,
        second_factor_matrix.T,
        coupling_matrix,
    )
    partial = pl.pallas_call(
        outer_kernel,
        out_shape=jax.ShapeDtypeStruct((pairs, pair_channels), F32),
        in_specs=[pl.BlockSpec(memory_space=pltpu.HBM)] * len(operands),
        out_specs=pl.BlockSpec(memory_space=pltpu.VMEM),
        scratch_shapes=[pltpu.VMEM(operand.shape, operand.dtype) for operand in operands] + [
            pltpu.SemaphoreType.DMA((len(operands),)),
            pltpu.VMEM((rows * residues // 2, 2 * channels), F32),
            pltpu.VMEM((rows * residues // 2 // LANES, 2 * hidden, LANES), F32),
            pltpu.VMEM((rows // hidden, pairs * hidden // LANES, LANES), F32),
            pltpu.VMEM((pairs, hidden * hidden), BF16),
        ],
        compiler_params=pltpu.CompilerParams(vmem_limit_bytes=48 * 1024 * 1024),
        name="outer_products",
    )(*(pltpu.with_memory_space_constraint(operand, pltpu.HBM) for operand in operands))
    refreshed_sequences = pl.pallas_call(
        transition_kernel,
        out_shape=jax.ShapeDtypeStruct(sequence_features.shape, BF16),
        compiler_params=pltpu.CompilerParams(vmem_limit_bytes=48 * 1024 * 1024),
        cost_estimate=pl.CostEstimate(flops=400_000_000, bytes_accessed=2_000_000, transcendentals=600_000),
        name="transition",
    )(
        sequence_features,
        row(feedforward_scale_vector),
        row(feedforward_shift_vector),
        feedforward_switch_matrix,
        feedforward_expand_matrix,
        feedforward_contract_matrix.T,
    )
    own = pairs // size
    if own % residues == 0:
        summed = scatter_sum(partial.reshape(size, own, pair_channels), size)
        summed = summed.reshape(own // residues, residues, pair_channels)
        counted = summed[:, residues - 1, :residues, None]
        last = lax.broadcasted_iota(jnp.int32, summed.shape, 1) == residues - 1
        summed = jnp.where(last, 0.0, summed)
        pair_mean_update = summed / jnp.maximum(counted, 1.0) + coupling_offset
    else:
        grid = partial.reshape(residues, residues, pair_channels)
        counted = lax.psum(grid[:, residues - 1, :residues], "rows").reshape(size, own)
        counted = pick(counted, lax.axis_index("rows"), 0)[:, None]
        last = lax.broadcasted_iota(jnp.int32, grid.shape, 1) == residues - 1
        summed = scatter_sum(jnp.where(last, 0.0, grid).reshape(size, own, pair_channels), size)
        pair_mean_update = summed / jnp.maximum(counted, 1.0) + coupling_offset
    return pair_mean_update.reshape(own, pair_channels), refreshed_sequences


def solution(mesh):
    everywhere = P()
    in_specs = (
        P(("groups", "rows"), None, None),
        P(("groups", "rows"), None),
        P("groups"),
    ) + (everywhere,) * 11
    out_specs = (P(("groups", "rows"), None), P(("groups", "rows"), None, None))
    return jax.shard_map(
        functools.partial(body, size=mesh.shape["rows"]),
        mesh=mesh, in_specs=in_specs, out_specs=out_specs, check_vma=False,
    )
```

time: 137 us -> 24.1 us (0.18)
  blocking collectives: 35.1 us -> 0 us
  local copies, waits for them, and re-layouts: 32.3 us -> 1.48 us
  waiting for transfers between devices: 35.6 us -> 5.03 us
  between operations: 14.8 us -> 0.78 us
  matrix products: 12.5 us -> 0 us
  starting transfers between devices: 0.04 us -> 8 us
  Pallas kernels: 0 us -> 7.83 us
  other arithmetic: 5.66 us -> 0.77 us
    reduce_scatter x1 -> x0, waiting for transfers between devices: 35.6 us -> none  [body(): lax.psum_scatter(outer, 'rows', scatter_dimension=0, tiled=True)]
    unnamed x1 -> x0, blocking collectives: 35.1 us -> none
    transpose x1 -> x0, local copies, waits for them, and re-layouts: 17.5 us -> none  [body(): jnp.einsum('sih,sjk->ijhk', left, right, preferred_element_type=jnp.float32)]
    reshape x2 -> x0, local copies, waits for them, and re-layouts: 13.7 us -> none  [the longest x1 13.7 us: body(): outer = outer.reshape(position_total * position_total, hidden * hidden)]
    dot_general x6 -> x0, matrix products: 12.5 us -> none  [the longest x1 7.32 us: body(): jnp.einsum('sih,sjk->ijhk', left, right, preferred_element_type=jnp.float32)]
    ppermute x0 -> x5, starting transfers between devices: none -> 8 us  [the longest x3 4.53 us: scatter_sum(): total = total + lax.ppermute(pick(partial, mine ^ k, 0), 'rows', partner)]
    pallas_call x0 -> x2, Pallas kernels: none -> 7.83 us  [the longest x1 4.5 us: body(): pl.pallas_call(outer_kernel, out_shape=jax.ShapeDtypeStruct((pairs, pair_...]
    ppermute x0 -> x5, waiting for transfers between devices: none -> 5.03 us  [the longest x2 4.86 us: scatter_sum(): lax.ppermute(pick(parts, 1 - mine, 1), 'rows', partner)]
  transfers between devices with their start and end apart: 1 -> 5, of which waited for: 1 -> 3; matrix products, arithmetic and copies ran while one was open for 3% -> 0% of each run, Pallas kernels for 0% -> 14%
where the time goes in v1:
time: 24.1 us; the launch traced here: 23.9 us
  starting transfers between devices  8 us (33%)
  Pallas kernels  7.83 us (32%)
  waiting for transfers between devices  5.03 us (21%)
  local copies, waits for them, and re-layouts  1.48 us (6%)
  between operations  0.78 us (3%)
  other arithmetic  0.77 us (3%)
    ppermute x2, waiting for transfers between devices, scatter_sum(): lax.ppermute(pick(parts, 1 - mine, 1), 'rows', partner)  4.86 us
    ppermute x3, starting transfers between devices, scatter_sum(): total = total + lax.ppermute(pick(partial, mine ^ k, 0), 'rows', partner)  4.53 us
    pallas_call x1, Pallas kernels, body(): pl.pallas_call(outer_kernel, out_shape=jax.ShapeDtypeStruct((pairs, pair_...  4.5 us
    ppermute x2, starting transfers between devices, scatter_sum(): lax.ppermute(pick(parts, 1 - mine, 1), 'rows', partner)  3.47 us
    pallas_call x1, Pallas kernels, body(): pl.pallas_call(transition_kernel, out_shape=jax.ShapeDtypeStruct(sequence...  3.33 us
    unnamed x14, local copies, waits for them, and re-layouts  1.24 us
    add x1, other arithmetic, body(): pair_mean_update = summed / jnp.maximum(counted, 1.0) + coupling_offset  0.7 us
  transfers between devices with their start and end apart: 5, of which 3 were waited for; matrix products, arithmetic and copies ran while one was open for 0% of the time, Pallas kernels for 14%

profile of v1, /device:TPU:0, one launch (start us, length us, event | category | flops | bytes accessed | tf_op | source)
XLA Modules:
  0.0 23.9 jit_solution(6271879606068548291)
XLA Ops:
  0.7 4.5 %outer_products.1 = f32[1024,128]{1,0:T(8,128)S(1)} custom-call(bf16[64,32,64]{2,1,0:T(8,128)(2,1)} %x_ref.1, s32[32,64]{1,0:T(8,128)} %bitcast.43, s32[1,32]{1,0:T(1,128)} %bitcast.47, f32[1,64]{1,0:T(1,128)} %bitcast.48, f32[1,64]{1,0:T(1,128)} %bitcast.49, bf16[32,64]{1,0:T(8,128)(2,1)} %bitcast.44, bf16[32,64]{1,0:T(8,128)(2,1)} %bitcast.45, ...), custom_call_target="tpu_custom_call" | custom-call | tf_op jit(solution)/shard_map/outer_products/pallas_call | solution.py:222
  5.2 0.5 %collective-permute-start = (f32[8,64,128]{2,1,0:T(8,128)S(1)}, f32[8,64,128]{2,1,0:T(8,128)S(1)}, u32[]{:S(2)}, u32[]{:S(2)}) collective-permute-start(f32[8,64,128]{2,1,0:T(8,128)S(1)} %dynamic-slice_bitcast_fusion), channel_id=1, source_target_pairs={{0,1},{1,0},{2,3},{3,2},{4,5},{5,4},{6,7},{7,6},{8,9},{9,8},{10,11... | collective-permute-start | bytes 786440 | tf_op jit(solution)/shard_map/ppermute | solution.py:179
  5.7 1.2 %collective-permute-done = f32[8,64,128]{2,1,0:T(8,128)S(1)} collective-permute-done((f32[8,64,128]{2,1,0:T(8,128)S(1)}, f32[8,64,128]{2,1,0:T(8,128)S(1)}, u32[]{:S(2)}, u32[]{:S(2)}) %collective-permute-start) | collective-permute-done | bytes 262176 | tf_op jit(solution)/shard_map/ppermute | solution.py:179
  6.9 0.0 copy-start
  6.9 3.0 %collective-permute-start.1 = (f32[4,64,128]{2,1,0:T(8,128)S(1)}, f32[4,64,128]{2,1,0:T(8,128)S(1)}, u32[]{:S(2)}, u32[]{:S(2)}) collective-permute-start(f32[4,64,128]{2,1,0:T(8,128)S(1)} %dynamic-slice_bitcast_fusion.1), channel_id=1, source_target_pairs={{0,2},{1,3},{2,0},{3,1},{4,6},{5,7},{6,4},{7,5},{8,10},{9,11},{10,... | collective-permute-start | bytes 393224 | tf_op jit(solution)/shard_map/ppermute | solution.py:179
  9.9 0.1 iota.12
  10.0 3.7 %collective-permute-done.1 = f32[4,64,128]{2,1,0:T(8,128)S(1)} collective-permute-done((f32[4,64,128]{2,1,0:T(8,128)S(1)}, f32[4,64,128]{2,1,0:T(8,128)S(1)}, u32[]{:S(2)}, u32[]{:S(2)}) %collective-permute-start.1) | collective-permute-done | bytes 131104 | tf_op jit(solution)/shard_map/ppermute | solution.py:179
  13.7 0.0 copy-start.1
  13.7 0.0 copy-start.2
  13.7 0.0 copy-start.3
  13.8 3.9 %collective-permute-start.4 = (f32[64,128]{1,0:T(8,128)S(1)}, f32[64,128]{1,0:T(8,128)S(1)}, u32[]{:S(2)}, u32[]{:S(2)}) collective-permute-start(f32[64,128]{1,0:T(8,128)S(1)} %get-tuple-element.3), channel_id=1, source_target_pairs={{0,12},{1,13},{2,14},{3,15},{4,8},{5,9},{6,10},{7,11},{8,4},{9,5},... | collective-permute-start | bytes 98312 | tf_op jit(solution)/shard_map/ppermute | solution.py:185
  17.7 0.0 collective-permute-start.3
  17.7 0.6 %collective-permute-start.2 = (f32[64,128]{1,0:T(8,128)S(1)}, f32[64,128]{1,0:T(8,128)S(1)}, u32[]{:S(2)}, u32[]{:S(2)}) collective-permute-start(f32[64,128]{1,0:T(8,128)S(1)} %get-tuple-element.2), channel_id=1, source_target_pairs={{0,4},{1,5},{2,6},{3,7},{4,0},{5,1},{6,2},{7,3},{8,12},{9,13},{10,... | collective-permute-start | bytes 98312 | tf_op jit(solution)/shard_map/ppermute | solution.py:185
  18.3 0.0 copy-start.4
  18.3 0.0 copy-start.5
  18.3 0.0 copy-done
  18.3 0.0 copy-done.1
  18.3 0.0 copy-done.2
  18.3 0.0 copy-done.3
  18.3 0.6 %copy-done.4 = f32[64]{0:T(128)S(1)} copy-done((f32[64]{0:T(128)S(1)}, f32[64]{0:T(128)}, u32[]{:S(2)}) %copy-start.4) | copy-done | bytes 280
  19.0 0.0 copy-done.5
  19.0 3.3 %transition.1 = bf16[64,32,64]{2,1,0:T(8,128)(2,1)} custom-call(bf16[64,32,64]{2,1,0:T(8,128)(2,1)S(1)} %copy-done, f32[1,64]{1,0:T(1,128)S(1)} %bitcast.38, f32[1,64]{1,0:T(1,128)S(1)} %bitcast.39, bf16[64,256]{1,0:T(8,128)(2,1)S(1)} %copy-done.1, bf16[64,256]{1,0:T(8,128)(2,1)S(1)} %copy-done.2, bf16[64,256]{1,0:T(8,128)(2,1)S(1)} %bitcast.37), custom_call_target="tpu_custom_call" | custom-call | flops 400000000 | bytes 2000000 | tf_op jit(solution)/shard_map/transition/pallas_call | solution.py:237
  22.3 0.0 collective-permute-done.4
  22.3 0.2 collective-permute-done.3
  22.5 0.0 collective-permute-done.2
  22.5 0.0 copy-start.6
  22.5 0.1 max.16
  22.6 0.6 %copy-done.6 = f32[128]{0:T(128)S(1)} copy-done((f32[128]{0:T(128)S(1)}, f32[128]{0:T(128)}, u32[]{:S(2)}) %copy-start.6) | copy-done | bytes 536
  23.2 0.7 %divide_add_fusion = f32[64,128]{1,0:T(8,128)} fusion(f32[64,128]{1,0:T(8,128)S(1)} %fusion.1, f32[128]{0:T(128)S(1)} %copy-done.6, f32[64]{0:T(128)S(1)} %max.16, pred[64]{0:T(512)(128)(4,1)S(1)} %iota.12), kind=kLoop, calls=%fused_computation.7 | loop fusion | flops 24576 | bytes 66368 | tf_op jit(solution)/shard_map/add | solution.py:258
  (10 shorter events, 0.1 us)
Async XLA Ops:
  5.2 1.7 %collective-permute-start = (f32[8,64,128]{2,1,0:T(8,128)S(1)}, f32[8,64,128]{2,1,0:T(8,128)S(1)}, u32[]{:S(2)}, u32[]{:S(2)}) collective-permute-start(f32[8,64,128]{2,1,0:T(8,128)S(1)} %dynamic-slice_bitcast_fusion), channel_id=1, source_target_pairs={{0,1},{1,0},{2,3},{3,2},{4,5},{5,4},{6,7},{7,6},{8,9},{9,8},{10,11... | collective-permute-start | bytes 786440 | tf_op jit(solution)/shard_map/ppermute | solution.py:179
  6.9 11.4 %copy-start = (bf16[64,32,64]{2,1,0:T(8,128)(2,1)S(1)}, bf16[64,32,64]{2,1,0:T(8,128)(2,1)}, u32[]{:S(2)}) copy-start(bf16[64,32,64]{2,1,0:T(8,128)(2,1)} %x_ref.1) | copy-start | bytes 786436
  6.9 6.8 %collective-permute-start.1 = (f32[4,64,128]{2,1,0:T(8,128)S(1)}, f32[4,64,128]{2,1,0:T(8,128)S(1)}, u32[]{:S(2)}, u32[]{:S(2)}) collective-permute-start(f32[4,64,128]{2,1,0:T(8,128)S(1)} %dynamic-slice_bitcast_fusion.1), channel_id=1, source_target_pairs={{0,2},{1,3},{2,0},{3,1},{4,6},{5,7},{6,4},{7,5},{8,10},{9,11},{10,... | collective-permute-start | bytes 393224 | tf_op jit(solution)/shard_map/ppermute | solution.py:179
  13.7 4.6 %copy-start.1 = (bf16[64,256]{1,0:T(8,128)(2,1)S(1)}, bf16[64,256]{1,0:T(8,128)(2,1)}, u32[]{:S(2)}) copy-start(bf16[64,256]{1,0:T(8,128)(2,1)} %switch_ref.1) | copy-start | bytes 98308
  13.7 4.6 %copy-start.2 = (bf16[64,256]{1,0:T(8,128)(2,1)S(1)}, bf16[64,256]{1,0:T(8,128)(2,1)}, u32[]{:S(2)}) copy-start(bf16[64,256]{1,0:T(8,128)(2,1)} %expand_ref.1) | copy-start | bytes 98308
  13.7 4.6 %copy-start.3 = (bf16[256,64]{0,1:T(8,128)(2,1)S(1)}, bf16[256,64]{0,1:T(8,128)(2,1)}, u32[]{:S(2)}) copy-start(bf16[256,64]{0,1:T(8,128)(2,1)} %param.27) | copy-start | bytes 98308
  13.8 8.5 %collective-permute-start.4 = (f32[64,128]{1,0:T(8,128)S(1)}, f32[64,128]{1,0:T(8,128)S(1)}, u32[]{:S(2)}, u32[]{:S(2)}) collective-permute-start(f32[64,128]{1,0:T(8,128)S(1)} %get-tuple-element.3), channel_id=1, source_target_pairs={{0,12},{1,13},{2,14},{3,15},{4,8},{5,9},{6,10},{7,11},{8,4},{9,5},... | collective-permute-start | bytes 98312 | tf_op jit(solution)/shard_map/ppermute | solution.py:185
  17.7 4.8 %collective-permute-start.3 = (f32[64,128]{1,0:T(8,128)S(1)}, f32[64,128]{1,0:T(8,128)S(1)}, u32[]{:S(2)}, u32[]{:S(2)}) collective-permute-start(f32[64,128]{1,0:T(8,128)S(1)} %get-tuple-element.4), channel_id=1, source_target_pairs={{0,8},{1,9},{2,10},{3,11},{4,12},{5,13},{6,14},{7,15},{8,0},{9,1},... | collective-permute-start | bytes 98312 | tf_op jit(solution)/shard_map/ppermute | solution.py:185
  17.7 4.8 %collective-permute-start.2 = (f32[64,128]{1,0:T(8,128)S(1)}, f32[64,128]{1,0:T(8,128)S(1)}, u32[]{:S(2)}, u32[]{:S(2)}) collective-permute-start(f32[64,128]{1,0:T(8,128)S(1)} %get-tuple-element.2), channel_id=1, source_target_pairs={{0,4},{1,5},{2,6},{3,7},{4,0},{5,1},{6,2},{7,3},{8,12},{9,13},{10,... | collective-permute-start | bytes 98312 | tf_op jit(solution)/shard_map/ppermute | solution.py:185
  18.3 0.7 %copy-start.4 = (f32[64]{0:T(128)S(1)}, f32[64]{0:T(128)}, u32[]{:S(2)}) copy-start(f32[64]{0:T(128)} %param.23) | copy-start | bytes 772
  18.3 0.7 %copy-start.5 = (f32[64]{0:T(128)S(1)}, f32[64]{0:T(128)}, u32[]{:S(2)}) copy-start(f32[64]{0:T(128)} %param.24) | copy-start | bytes 772
  22.5 0.7 %copy-start.6 = (f32[128]{0:T(128)S(1)}, f32[128]{0:T(128)}, u32[]{:S(2)}) copy-start(f32[128]{0:T(128)} %param.22) | copy-start | bytes 1540

commit v2 on v1

v2 whole, which is shorter than its diff:
```python
import functools

import jax
import jax.numpy as jnp
from jax import lax
from jax.experimental import pallas as pl
from jax.experimental.pallas import tpu as pltpu
from jax.sharding import PartitionSpec as P

F32 = jnp.float32
BF16 = jnp.bfloat16
EPS = 1e-05
LANES = 128
VMEM_LIMIT = 48 * 1024 * 1024
STEP = 16
OWNERS = 16


def dot(a, b, dims=((1,), (0,))):
    return lax.dot_general(a, b, (dims, ((), ())), preferred_element_type=F32)


def two_halves(array, half):
    return jnp.concatenate([array[:, :half, :], array[:, half:, :]], axis=-1)


def twice(vector):
    return jnp.concatenate([vector, vector], axis=-1)


def block_pair(matrix):
    zero = jnp.zeros_like(matrix)
    return jnp.concatenate(
        [jnp.concatenate([matrix, zero], axis=1), jnp.concatenate([zero, matrix], axis=1)], axis=0
    )


def iota(shape, axis):
    return lax.broadcasted_iota(jnp.int32, shape, axis)


def mean_matrix(channels):
    shape = (2 * channels, 2 * channels)
    same = iota(shape, 0) // channels == iota(shape, 1) // channels
    return jnp.where(same, 1.0 / channels, 0.0).astype(BF16)


def standardize_pairs(values, averaging, gain, bias):
    centered = values.astype(F32) - dot(values, averaging)
    variance = dot((centered * centered).astype(BF16), averaging)
    return centered * lax.rsqrt(variance + EPS) * gain + bias


def place(residue, me, per_owner):
    if me is None:
        return residue
    apart = (residue // per_owner) ^ me
    rank = (apart & 1) * 8 + ((apart >> 1) & 1) * 4 + ((apart >> 2) ^ 2)
    return rank * per_owner + residue % per_owner


def outer_kernel(relative, n_inputs, n_handed, *refs):
    sources = refs[:n_inputs]
    keep_ref, send_ref = refs[n_inputs : n_inputs + 2]
    handed = refs[n_inputs + 2 : n_inputs + 2 + n_handed]
    own = n_inputs - n_handed
    targets = refs[n_inputs + 2 + n_handed :][:own]
    arrived, x_scratch, left_t_scratch, left_scratch, x_mat = refs[n_inputs + 2 + n_handed + own :]
    presence_ref, position_ref, gain_ref, bias_ref, first_ref, second_ref, coupling_ref = targets
    x_ref = handed[0]
    me = lax.axis_index("rows") if relative else None
    order = (handed[0],) + tuple(targets) + tuple(handed[1:])
    copies = [
        pltpu.make_async_copy(source, target, arrived.at[n])
        for n, (source, target) in enumerate(zip(sources, order))
    ]
    for copy in copies:
        copy.start()
    rows, residues, channels = x_ref.shape
    hidden = first_ref.shape[0]
    half = residues // 2
    per_owner = residues // OWNERS
    quad = LANES // hidden
    groups = hidden // quad
    square = (residues, residues)

    for copy in copies[:own]:
        copy.wait()
    x_scratch[...] = two_halves(x_ref[...], half).astype(F32).reshape(rows * half, 2 * channels)
    tokens = jnp.concatenate(
        [x_scratch[pl.ds(p, rows, stride=half), :] for p in range(half)], axis=0
    ).astype(BF16)
    normed = standardize_pairs(tokens, mean_matrix(channels), twice(gain_ref[...]), twice(bias_ref[...]))

    diagonal = iota(square, 0) == iota(square, 1)
    position = jnp.where(diagonal, position_ref[...].astype(F32), 0.0).sum(axis=1, keepdims=True)
    valid = (presence_ref[...].astype(F32) * position).astype(BF16)
    lanes = iota((residues, half * 2 * channels), 1)
    wanted = lanes // (2 * channels) + half * ((lanes % (2 * channels)) // channels)
    spread = jnp.where(iota(lanes.shape, 0) == wanted, 1.0, 0.0).astype(BF16)
    flags = dot(valid, spread, ((0,), (0,)))
    flags = jnp.concatenate(
        [flags[:, p * 2 * channels : (p + 1) * 2 * channels] for p in range(half)], axis=0
    )
    normed = (normed * flags).astype(BF16)

    left_t = dot(block_pair(first_ref[...]), normed, ((1,), (1,)))
    for v in range(left_t_scratch.shape[0]):
        left_t_scratch[v] = left_t[:, v * LANES : (v + 1) * LANES]
    low = iota((groups, LANES), 1) < rows
    per = LANES // rows
    for side in range(2):
        for v in range(half // per):
            pieces = [
                left_t_scratch[v, pl.ds(side * hidden + h4, groups, stride=quad), :]
                for h4 in range(quad)
            ]
            turned = [pltpu.roll(piece, rows, 1) for piece in pieces]
            for odd in range(2):
                row = place(side * half + v * per + odd, me, per_owner)
                for c in range(quad // 2):
                    if odd:
                        tile = jnp.where(low, turned[2 * c], pieces[2 * c + 1])
                    else:
                        tile = jnp.where(low, pieces[2 * c], turned[2 * c + 1])
                    left_scratch[c, pl.ds(row, groups, stride=residues), :] = tile
    left = jnp.concatenate(
        [left_scratch[c] for c in range(quad // 2)], axis=1
    ).astype(BF16)

    repeated = jnp.concatenate([second_ref[...]] * quad, axis=0)
    right = dot(normed, block_pair(repeated), ((1,), (1,))).astype(BF16)
    lane_group = iota((rows, LANES), 1) // hidden
    masks = [lane_group == h4 for h4 in range(quad)]
    zero = jnp.zeros((rows, LANES), BF16)
    for j in range(residues):
        side, p = j // half, j % half
        one = right[p * rows : (p + 1) * rows, side * LANES : (side + 1) * LANES]
        spread_right = jnp.concatenate([jnp.where(m, one, zero) for m in masks], axis=0)
        product = dot(left, spread_right).astype(BF16)
        for g in range(groups):
            x_mat[j * residues : (j + 1) * residues, g * LANES : (g + 1) * LANES] = product[
                g * residues : (g + 1) * residues, :
            ]
    copies[own].wait()
    projected = dot(x_mat[...], coupling_ref[...])
    order = (place(iota(square, 1), me, per_owner) == iota(square, 0)).astype(BF16)
    counts = dot(dot(order, valid).astype(BF16), valid, ((1,), (1,)))
    counts = jnp.concatenate([counts, jnp.zeros((residues, LANES - residues), F32)], axis=1)
    for j in range(residues):
        rows_j = counts if j == residues - 1 else projected[j * residues : (j + 1) * residues, :]
        keep_ref[pl.ds(j, half, stride=residues), :] = rows_j[:half]
        send_ref[pl.ds(j, half, stride=residues), :] = rows_j[half:]
    for copy in copies[own + 1 :]:
        copy.wait()


def transition_rows(x_ref, start, count, gain_ref, bias_ref, switch_ref, expand_ref, contract_ref, out_ref):
    _, residues, channels = x_ref.shape
    half = residues // 2
    averaging = mean_matrix(channels)
    gain, bias = twice(gain_ref[...]), twice(bias_ref[...])
    switch = block_pair(switch_ref[...])
    expand = block_pair(expand_ref[...])
    contract = block_pair(contract_ref[...])
    for at in range(0, count, STEP):
        pairs = two_halves(x_ref[start + at : start + at + STEP], half).reshape(STEP * half, 2 * channels)
        normed = standardize_pairs(pairs, averaging, gain, bias).astype(BF16)
        gate = dot(normed, switch) * 0.5
        inner = ((gate + gate * jnp.tanh(gate)) * dot(normed, expand)).astype(BF16)
        result = (pairs.astype(F32) + dot(inner, contract, ((1,), (1,)))).astype(BF16)
        result = result.reshape(STEP, half, 2 * channels)
        out_ref[at : at + STEP, :half, :] = result[:, :, :channels]
        out_ref[at : at + STEP, half:, :] = result[:, :, channels:]
        yield at


def transition_head(x_ref, *refs):
    *weight_refs, out_ref = refs
    for _ in transition_rows(x_ref, 0, out_ref.shape[0], *weight_refs, out_ref):
        pass


def transition_tail(x_ref, *refs):
    *weight_refs, head_ref, out_hbm, result_ref, sent = refs
    head = head_ref.shape[0]
    copies = [pltpu.make_async_copy(head_ref, out_hbm.at[pl.ds(0, head)], sent.at[0])]
    copies[0].start()
    for at in transition_rows(x_ref, head, result_ref.shape[0], *weight_refs, result_ref):
        copies.append(
            pltpu.make_async_copy(
                result_ref.at[pl.ds(at, STEP)], out_hbm.at[pl.ds(head + at, STEP)], sent.at[len(copies)]
            )
        )
        copies[-1].start()
    for copy in copies:
        copy.wait()


def finish_kernel(residues, *refs):
    *summand_refs, offset_ref, out_ref = refs
    total = summand_refs[0][...]
    for ref in summand_refs[1:]:
        total = total + ref[...]
    square = (residues, residues)
    diagonal = iota(square, 0) == iota(square, 1)
    last = iota((residues, total.shape[1]), 0) == residues - 1
    for start in range(0, total.shape[0], residues):
        block = total[start : start + residues]
        counts = jnp.where(diagonal, block[residues - 1 :, :residues], 0.0).sum(axis=1, keepdims=True)
        mean = jnp.where(last, 0.0, block) / jnp.maximum(counts, 1.0)
        out_ref[start : start + residues, :] = mean + offset_ref[...]


def pick(array, index, axis):
    return lax.dynamic_index_in_dim(array, index, axis, keepdims=False)


def swap(array, size, apart):
    return lax.ppermute(array, "rows", [(i, i ^ apart) for i in range(size)])


def scatter_sum(partial, size):
    me = lax.axis_index("rows")
    tail = partial.shape[1:]
    done = 1
    while size // done > 4 or (size // done) % 4:
        parts = partial.reshape((size // done // 2, 2) + tail)
        mine = (me // done) % 2
        partial = pick(parts, mine, 1) + swap(pick(parts, 1 - mine, 1), size, done)
        done *= 2
    mine = me // done
    total = pick(partial, mine, 0)
    for k in range(1, size // done):
        total = total + swap(pick(partial, mine ^ k, 0), size, k * done)
    return total


def inside(shape, dtype):
    return pltpu.VMEM(shape, dtype)


def transition(features, weights, head_rows):
    rows, residues, channels = features.shape
    vmem = pl.BlockSpec(memory_space=pltpu.VMEM)
    cost = lambda count: pl.CostEstimate(
        flops=6_000_000 * count, bytes_accessed=30_000 * count, transcendentals=8_000 * count
    )
    params = pltpu.CompilerParams(vmem_limit_bytes=VMEM_LIMIT)
    pinned = [pltpu.with_memory_space_constraint(a, pltpu.VMEM) for a in (features,) + tuple(weights)]
    head = lambda: pl.pallas_call(
        transition_head,
        out_shape=inside((head_rows, residues, channels), BF16),
        in_specs=[vmem] * len(pinned),
        out_specs=vmem,
        compiler_params=params,
        cost_estimate=cost(head_rows),
        name="transition_head",
    )(*pinned)
    tail = lambda before: pl.pallas_call(
        transition_tail,
        out_shape=jax.ShapeDtypeStruct(features.shape, BF16),
        in_specs=[vmem] * (len(pinned) + 1),
        out_specs=pl.BlockSpec(memory_space=pltpu.HBM),
        scratch_shapes=[
            pltpu.VMEM((rows - head_rows, residues, channels), BF16),
            pltpu.SemaphoreType.DMA((1 + (rows - head_rows) // STEP,)),
        ],
        compiler_params=params,
        cost_estimate=cost(rows - head_rows),
        name="transition_tail",
    )(*pinned, pltpu.with_memory_space_constraint(before, pltpu.VMEM))
    return head, tail


def body(
    sequence_features,
    sequence_presence,
    position_presence,
    product_scale_vector,
    product_shift_vector,
    first_factor_matrix,
    second_factor_matrix,
    coupling_matrix,
    coupling_offset,
    feedforward_scale_vector,
    feedforward_shift_vector,
    feedforward_switch_matrix,
    feedforward_expand_matrix,
    feedforward_contract_matrix,
    *,
    size,
):
    rows, residues, channels = sequence_features.shape
    hidden = first_factor_matrix.shape[1]
    pair_channels = coupling_matrix.shape[1]
    pairs = residues * residues
    own = pairs // size
    relative = size == OWNERS
    row = lambda v: v.reshape(1, -1)
    used = (
        sequence_presence.T,
        row(position_presence),
        row(product_scale_vector),
        row(product_shift_vector),
        first_factor_matrix.T,
        second_factor_matrix.T,
        coupling_matrix,
    )
    handed = (
        sequence_features,
        row(coupling_offset),
        row(feedforward_scale_vector),
        row(feedforward_shift_vector),
        feedforward_switch_matrix,
        feedforward_expand_matrix,
        feedforward_contract_matrix.T,
    )
    operands = handed[:1] + used + handed[1:]
    results = [inside((pairs // 2, pair_channels), F32)] * 2
    results += [inside(operand.shape, operand.dtype) for operand in handed]
    keep, send, features, offset, *weights = pl.pallas_call(
        functools.partial(outer_kernel, relative, len(operands), len(handed)),
        out_shape=results,
        in_specs=[pl.BlockSpec(memory_space=pltpu.HBM)] * len(operands),
        out_specs=[pl.BlockSpec(memory_space=pltpu.VMEM)] * len(results),
        scratch_shapes=[pltpu.VMEM(operand.shape, operand.dtype) for operand in used] + [
            pltpu.SemaphoreType.DMA((len(operands),)),
            pltpu.VMEM((rows * residues // 2, 2 * channels), F32),
            pltpu.VMEM((rows * residues // 2 // LANES, 2 * hidden, LANES), F32),
            pltpu.VMEM((rows // hidden, pairs * hidden // LANES, LANES), F32),
            pltpu.VMEM((pairs, hidden * hidden), BF16),
        ],
        compiler_params=pltpu.CompilerParams(vmem_limit_bytes=VMEM_LIMIT),
        name="outer_products",
    )(*(pltpu.with_memory_space_constraint(operand, pltpu.HBM) for operand in operands))
    head, tail = transition(features, weights, rows // 4)
    if relative:
        keep = keep.reshape(2, 4, own, pair_channels)
        head_rows = head()
        got, head_rows = lax.optimization_barrier((swap(send, size, 1), head_rows))
        got = got.reshape(2, 4, own, pair_channels)
        away = keep[1] + got[1]
        far = swap(away[:2], size, 2)
        near = swap(away[2:], size, 2)
        here = keep[0] + got[0]
        upper = here[:2] + far
        two, three = swap(upper[0], size, 8), swap(upper[1], size, 12)
        lower = here[2:] + near
        one = swap(lower[1], size, 4)
        refreshed = tail(head_rows)
        summands = (two, three, one, lower[0])
        pair_mean_update = pl.pallas_call(
            functools.partial(finish_kernel, residues),
            out_shape=jax.ShapeDtypeStruct((own, pair_channels), F32),
            in_specs=[pl.BlockSpec(memory_space=pltpu.VMEM)] * (len(summands) + 1),
            compiler_params=pltpu.CompilerParams(vmem_limit_bytes=VMEM_LIMIT),
            name="finish",
        )(*(pltpu.with_memory_space_constraint(a, pltpu.VMEM) for a in summands + (offset,)))
    else:
        refreshed = tail(head())
        grid = jnp.concatenate([keep.reshape(residues // 2, residues, pair_channels),
                                send.reshape(residues // 2, residues, pair_channels)], axis=0)
        counted = lax.psum(grid[:, residues - 1, :residues], "rows").reshape(size, own)
        counted = pick(counted, lax.axis_index("rows"), 0)[:, None]
        last = iota(grid.shape, 1) == residues - 1
        summed = scatter_sum(jnp.where(last, 0.0, grid).reshape(size, own, pair_channels), size)
        pair_mean_update = summed / jnp.maximum(counted, 1.0) + coupling_offset
    return pair_mean_update, refreshed


def solution(mesh):
    in_specs = (
        P(("groups", "rows"), None, None),
        P(("groups", "rows"), None),
        P("groups"),
    ) + (P(),) * 11
    out_specs = (P(("groups", "rows"), None), P(("groups", "rows"), None, None))
    return jax.shard_map(
        functools.partial(body, size=mesh.shape["rows"]),
        mesh=mesh, in_specs=in_specs, out_specs=out_specs, check_vma=False,
    )
```

time: 24.1 us -> 22.4 us (0.929)
  local copies, waits for them, and re-layouts: 1.48 us -> 0.03 us
  waiting for transfers between devices: 5.03 us -> 4.03 us
  Pallas kernels: 7.83 us -> 8.8 us
  other arithmetic: 0.77 us -> 0.06 us
  starting transfers between devices: 8 us -> 8.59 us
    unnamed x14 -> x0, local copies, waits for them, and re-layouts: 1.24 us -> none
    ppermute x5 -> x6, waiting for transfers between devices: 5.03 us -> 4.03 us  [swap(): return lax.ppermute(array, 'rows', [(i, i ^ apart) for i in range(size)])]
    pallas_call x2 -> x4, Pallas kernels: 7.83 us -> 8.8 us  [the longest x1 4.61 us: body(): pl.pallas_call(functools.partial(outer_kernel, relative, len(operands), l...]
    add x4 -> x3, other arithmetic: 0.76 us -> 0.06 us  [the longest x1 0.04 us: body(): away = keep[1] + got[1]]
    ppermute x5 -> x6, starting transfers between devices: 8 us -> 8.59 us  [swap(): return lax.ppermute(array, 'rows', [(i, i ^ apart) for i in range(size)])]
  transfers between devices with their start and end apart: 5 -> 6, of which waited for: 3 -> 3; matrix products, arithmetic and copies ran while one was open for 0% -> 0% of each run, Pallas kernels for 14% -> 16%
where the time goes in v2:
time: 22.4 us; the launch traced here: 22.2 us
  Pallas kernels  8.8 us (39%)
  starting transfers between devices  8.59 us (38%)
  waiting for transfers between devices  4.03 us (18%)
  between operations  0.7 us (3%)
    ppermute x6, starting transfers between devices, swap(): return lax.ppermute(array, 'rows', [(i, i ^ apart) for i in range(size)])  8.59 us
    pallas_call x1, Pallas kernels, body(): pl.pallas_call(functools.partial(outer_kernel, relative, len(operands), l...  4.61 us
    ppermute x6, waiting for transfers between devices, swap(): return lax.ppermute(array, 'rows', [(i, i ^ apart) for i in range(size)])  4.03 us
    pallas_call x1, Pallas kernels, transition(): pl.pallas_call(transition_tail, out_shape=jax.ShapeDtypeStruct(features.s...  2.66 us
    pallas_call x1, Pallas kernels, transition(): pl.pallas_call(transition_head, out_shape=inside((head_rows, residues, ch...  0.82 us
    pallas_call x1, Pallas kernels, body(): pl.pallas_call(functools.partial(finish_kernel, residues), out_shape=jax....  0.72 us
  transfers between devices with their start and end apart: 6, of which 3 were waited for; matrix products, arithmetic and copies ran while one was open for 0% of the time, Pallas kernels for 16%

profile of v2, /device:TPU:0, one launch (start us, length us, event | category | flops | bytes accessed | tf_op | source)
XLA Modules:
  0.0 22.2 jit_solution(12520403703910328908)
XLA Ops:
  0.6 4.6 %outer_products.1 = (f32[512,128]{1,0:T(8,128)S(1)}, f32[512,128]{1,0:T(8,128)S(1)}, bf16[64,32,64]{2,1,0:T(8,128)(2,1)S(1)}, f32[1,128]{1,0:T(1,128)S(1)}, f32[...) custom-call(bf16[64,32,64]{2,1,0:T(8,128)(2,1)} %refs_0_.1, ...), custom_call_target="tpu_custom_call" | custom-call | tf_op jit(solution)/shard_map/outer_products/pallas_call | solution.py:322
  5.3 0.5 %collective-permute-start = (f32[512,128]{1,0:T(8,128)S(1)}, f32[512,128]{1,0:T(8,128)S(1)}, u32[]{:S(2)}, u32[]{:S(2)}) collective-permute-start(f32[512,128]{1,0:T(8,128)S(1)} %get-tuple-element.14), channel_id=1, source_target_pairs={{0,1},{1,0},{2,3},{3,2},{4,5},{5,4},{6,7},{7,6},{8,9},{9,8},{10,11... | collective-permute-start | bytes 786440 | tf_op jit(solution)/shard_map/ppermute | solution.py:220
  5.8 0.8 %transition_head.1.refs_5_ = bf16[16,32,64]{2,1,0:T(8,128)(2,1)S(1)} custom-call(bf16[64,32,64]{2,1,0:T(8,128)(2,1)S(1)} %get-tuple-element.15.x_ref, f32[1,64]{1,0:T(1,128)S(1)} %get-tuple-element.16.refs_0_, f32[1,64]{1,0:T(1,128)S(1)} %get-tuple-element.17.refs_1_, bf16[64,256]{1,0:T(8,128)(2,1)S(1)} %get-tuple-element.18.refs_2_, ...), custom_call_target="tpu_custom_call" | custom-call | flops 96000000 | bytes 480000 | tf_op jit(solution)/shard_map/transition_head/pallas_call | solution.py:251
  6.6 0.3 %collective-permute-done = f32[512,128]{1,0:T(8,128)S(1)} collective-permute-done((f32[512,128]{1,0:T(8,128)S(1)}, f32[512,128]{1,0:T(8,128)S(1)}, u32[]{:S(2)}, u32[]{:S(2)}) %collective-permute-start) | collective-permute-done | bytes 262176 | tf_op jit(solution)/shard_map/ppermute | solution.py:220
  7.0 3.0 %collective-permute-start.1 = (f32[2,64,128]{2,1,0:T(8,128)S(1)}, f32[2,64,128]{2,1,0:T(8,128)S(1)}, u32[]{:S(2)}, u32[]{:S(2)}) collective-permute-start(f32[2,64,128]{2,1,0:T(8,128)S(1)} %bitcast.25), channel_id=1, source_target_pairs={{0,2},{1,3},{2,0},{3,1},{4,6},{5,7},{6,4},{7,5},{8,10},{9,11},{10,... | collective-permute-start | bytes 196616 | tf_op jit(solution)/shard_map/ppermute | solution.py:220
  10.0 0.1 collective-permute-start.4
  10.0 2.3 %collective-permute-done.1 = f32[2,64,128]{2,1,0:T(8,128)S(1)} collective-permute-done((f32[2,64,128]{2,1,0:T(8,128)S(1)}, f32[2,64,128]{2,1,0:T(8,128)S(1)}, u32[]{:S(2)}, u32[]{:S(2)}) %collective-permute-start.1) | collective-permute-done | bytes 65568 | tf_op jit(solution)/shard_map/ppermute | solution.py:220
  12.4 3.4 %collective-permute-start.2 = (f32[64,128]{1,0:T(8,128)S(1)}, f32[64,128]{1,0:T(8,128)S(1)}, u32[]{:S(2)}, u32[]{:S(2)}) collective-permute-start(f32[64,128]{1,0:T(8,128)S(1)} %get-tuple-element.33), channel_id=1, source_target_pairs={{0,8},{1,9},{2,10},{3,11},{4,12},{5,13},{6,14},{7,15},{8,0},{9,1},... | collective-permute-start | bytes 98312 | tf_op jit(solution)/shard_map/ppermute | solution.py:220
  15.8 1.3 %collective-permute-start.3 = (f32[64,128]{1,0:T(8,128)S(1)}, f32[64,128]{1,0:T(8,128)S(1)}, u32[]{:S(2)}, u32[]{:S(2)}) collective-permute-start(f32[64,128]{1,0:T(8,128)S(1)} %get-tuple-element.32), channel_id=1, source_target_pairs={{0,12},{1,13},{2,14},{3,15},{4,8},{5,9},{6,10},{7,11},{8,4},{9,5},... | collective-permute-start | bytes 98312 | tf_op jit(solution)/shard_map/ppermute | solution.py:220
  17.1 0.0 collective-permute-done.4
  17.1 0.3 %collective-permute-start.5 = (f32[64,128]{1,0:T(8,128)S(1)}, f32[64,128]{1,0:T(8,128)S(1)}, u32[]{:S(2)}, u32[]{:S(2)}) collective-permute-start(f32[64,128]{1,0:T(8,128)S(1)} %get-tuple-element.31), channel_id=1, source_target_pairs={{0,4},{1,5},{2,6},{3,7},{4,0},{5,1},{6,2},{7,3},{8,12},{9,13},{10,... | collective-permute-start | bytes 98312 | tf_op jit(solution)/shard_map/ppermute | solution.py:220
  17.5 2.7 %transition_tail.1 = bf16[64,32,64]{2,1,0:T(8,128)(2,1)} custom-call(bf16[64,32,64]{2,1,0:T(8,128)(2,1)S(1)} %get-tuple-element.15.x_ref, f32[1,64]{1,0:T(1,128)S(1)} %get-tuple-element.16.refs_0_, f32[1,64]{1,0:T(1,128)S(1)} %get-tuple-element.17.refs_1_, bf16[64,256]{1,0:T(8,128)(2,1)S(1)} %get-tuple-element.18.refs_2_, ...), custom_call_target="tpu_custom_call" | custom-call | flops 288000000 | bytes 1440000 | tf_op jit(solution)/shard_map/transition_tail/pallas_call | solution.py:260
  20.1 0.0 collective-permute-done.2.refs_0_
  20.1 1.4 %collective-permute-done.3.refs_1_ = f32[64,128]{1,0:T(8,128)S(1)} collective-permute-done((f32[64,128]{1,0:T(8,128)S(1)}, f32[64,128]{1,0:T(8,128)S(1)}, u32[]{:S(2)}, u32[]{:S(2)}) %collective-permute-start.3) | collective-permute-done | bytes 32800 | tf_op jit(solution)/shard_map/ppermute | solution.py:220
  21.5 0.0 collective-permute-done.5.refs_2_
  21.5 0.7 %finish.1 = f32[64,128]{1,0:T(8,128)} custom-call(f32[64,128]{1,0:T(8,128)S(1)} %collective-permute-done.2.refs_0_, f32[64,128]{1,0:T(8,128)S(1)} %collective-permute-done.3.refs_1_, f32[64,128]{1,0:T(8,128)S(1)} %collective-permute-done.5.refs_2_, f32[64,128]{1,0:T(8,128)S(1)} %get-tuple-element.30.refs_3_, f32[1,128]{1,0:T(1,128)S(1)} %get-tuple-element.22.refs_4_), custom_call_target="tpu_custom_call" | custom-call | tf_op jit(solution)/shard_map/finish/pallas_call | solution.py:353
  (6 shorter events, 0.1 us)
Async XLA Ops:
  5.3 1.7 %collective-permute-start = (f32[512,128]{1,0:T(8,128)S(1)}, f32[512,128]{1,0:T(8,128)S(1)}, u32[]{:S(2)}, u32[]{:S(2)}) collective-permute-start(f32[512,128]{1,0:T(8,128)S(1)} %get-tuple-element.14), channel_id=1, source_target_pairs={{0,1},{1,0},{2,3},{3,2},{4,5},{5,4},{6,7},{7,6},{8,9},{9,8},{10,11... | collective-permute-start | bytes 786440 | tf_op jit(solution)/shard_map/ppermute | solution.py:220
  7.0 5.3 %collective-permute-start.1 = (f32[2,64,128]{2,1,0:T(8,128)S(1)}, f32[2,64,128]{2,1,0:T(8,128)S(1)}, u32[]{:S(2)}, u32[]{:S(2)}) collective-permute-start(f32[2,64,128]{2,1,0:T(8,128)S(1)} %bitcast.25), channel_id=1, source_target_pairs={{0,2},{1,3},{2,0},{3,1},{4,6},{5,7},{6,4},{7,5},{8,10},{9,11},{10,... | collective-permute-start | bytes 196616 | tf_op jit(solution)/shard_map/ppermute | solution.py:220
  10.0 7.2 %collective-permute-start.4 = (f32[2,64,128]{2,1,0:T(8,128)S(1)}, f32[2,64,128]{2,1,0:T(8,128)S(1)}, u32[]{:S(2)}, u32[]{:S(2)}) collective-permute-start(f32[2,64,128]{2,1,0:T(8,128)S(1)} %bitcast.24), channel_id=1, source_target_pairs={{0,2},{1,3},{2,0},{3,1},{4,6},{5,7},{6,4},{7,5},{8,10},{9,11},{10,... | collective-permute-start | bytes 196616 | tf_op jit(solution)/shard_map/ppermute | solution.py:220
  12.4 7.7 %collective-permute-start.2 = (f32[64,128]{1,0:T(8,128)S(1)}, f32[64,128]{1,0:T(8,128)S(1)}, u32[]{:S(2)}, u32[]{:S(2)}) collective-permute-start(f32[64,128]{1,0:T(8,128)S(1)} %get-tuple-element.33), channel_id=1, source_target_pairs={{0,8},{1,9},{2,10},{3,11},{4,12},{5,13},{6,14},{7,15},{8,0},{9,1},... | collective-permute-start | bytes 98312 | tf_op jit(solution)/shard_map/ppermute | solution.py:220
  15.8 5.7 %collective-permute-start.3 = (f32[64,128]{1,0:T(8,128)S(1)}, f32[64,128]{1,0:T(8,128)S(1)}, u32[]{:S(2)}, u32[]{:S(2)}) collective-permute-start(f32[64,128]{1,0:T(8,128)S(1)} %get-tuple-element.32), channel_id=1, source_target_pairs={{0,12},{1,13},{2,14},{3,15},{4,8},{5,9},{6,10},{7,11},{8,4},{9,5},... | collective-permute-start | bytes 98312 | tf_op jit(solution)/shard_map/ppermute | solution.py:220
  17.1 4.4 %collective-permute-start.5 = (f32[64,128]{1,0:T(8,128)S(1)}, f32[64,128]{1,0:T(8,128)S(1)}, u32[]{:S(2)}, u32[]{:S(2)}) collective-permute-start(f32[64,128]{1,0:T(8,128)S(1)} %get-tuple-element.31), channel_id=1, source_target_pairs={{0,4},{1,5},{2,6},{3,7},{4,0},{5,1},{6,2},{7,3},{8,12},{9,13},{10,... | collective-permute-start | bytes 98312 | tf_op jit(solution)/shard_map/ppermute | solution.py:220

commit v3 on v2

--- a/solution.py
+++ b/solution.py
@@ -13,6 +13,10 @@
 LANES = 128
 VMEM_LIMIT = 48 * 1024 * 1024
 STEP = 16
+JOIN = 2
+CHUNK = 512
+FIRST_HOP = (2, 3, 1, 0)
+SECOND_HOP = (3, 2, 0, 1)
 OWNERS = 16
 
 
@@ -55,7 +59,9 @@
     if me is None:
         return residue
     apart = (residue // per_owner) ^ me
-    rank = (apart & 1) * 8 + ((apart >> 1) & 1) * 4 + ((apart >> 2) ^ 2)
+    along = apart >> 2
+    swapped = (along >> 1) & (me >> 3)
+    rank = (apart & 1) * 8 + ((apart >> 1) & 1) * 4 + ((along ^ 2) ^ swapped)
     return rank * per_owner + residue % per_owner
 
 
@@ -74,7 +80,7 @@
         pltpu.make_async_copy(source, target, arrived.at[n])
         for n, (source, target) in enumerate(zip(sources, order))
     ]
-    for copy in copies:
+    for copy in copies[: own + 1]:
         copy.start()
     rows, residues, channels = x_ref.shape
     hidden = first_ref.shape[0]
@@ -84,20 +90,25 @@
     groups = hidden // quad
     square = (residues, residues)
 
-    for copy in copies[:own]:
+    averaging = mean_matrix(channels)
+    lanes = iota((residues, half * 2 * channels), 1)
+    wanted = lanes // (2 * channels) + half * ((lanes % (2 * channels)) // channels)
+    spread = jnp.where(iota(lanes.shape, 0) == wanted, 1.0, 0.0).astype(BF16)
+    diagonal = iota(square, 0) == iota(square, 1)
+    order = (place(iota(square, 1), me, per_owner) == iota(square, 0)).astype(BF16)
+
+    for copy in copies[own + 1 :]:
+        copy.start()
+    for copy in copies[: own + 1]:
         copy.wait()
     x_scratch[...] = two_halves(x_ref[...], half).astype(F32).reshape(rows * half, 2 * channels)
     tokens = jnp.concatenate(
         [x_scratch[pl.ds(p, rows, stride=half), :] for p in range(half)], axis=0
     ).astype(BF16)
-    normed = standardize_pairs(tokens, mean_matrix(channels), twice(gain_ref[...]), twice(bias_ref[...]))
-
-    diagonal = iota(square, 0) == iota(square, 1)
+    normed = standardize_pairs(tokens, averaging, twice(gain_ref[...]), twice(bias_ref[...]))
+
     position = jnp.where(diagonal, position_ref[...].astype(F32), 0.0).sum(axis=1, keepdims=True)
     valid = (presence_ref[...].astype(F32) * position).astype(BF16)
-    lanes = iota((residues, half * 2 * channels), 1)
-    wanted = lanes // (2 * channels) + half * ((lanes % (2 * channels)) // channels)
-    spread = jnp.where(iota(lanes.shape, 0) == wanted, 1.0, 0.0).astype(BF16)
     flags = dot(valid, spread, ((0,), (0,)))
     flags = jnp.concatenate(
         [flags[:, p * 2 * channels : (p + 1) * 2 * channels] for p in range(half)], axis=0
@@ -133,18 +144,24 @@
     lane_group = iota((rows, LANES), 1) // hidden
     masks = [lane_group == h4 for h4 in range(quad)]
     zero = jnp.zeros((rows, LANES), BF16)
-    for j in range(residues):
-        side, p = j // half, j % half
-        one = right[p * rows : (p + 1) * rows, side * LANES : (side + 1) * LANES]
-        spread_right = jnp.concatenate([jnp.where(m, one, zero) for m in masks], axis=0)
-        product = dot(left, spread_right).astype(BF16)
-        for g in range(groups):
-            x_mat[j * residues : (j + 1) * residues, g * LANES : (g + 1) * LANES] = product[
-                g * residues : (g + 1) * residues, :
-            ]
-    copies[own].wait()
-    projected = dot(x_mat[...], coupling_ref[...])
-    order = (place(iota(square, 1), me, per_owner) == iota(square, 0)).astype(BF16)
+    for j in range(0, residues, JOIN):
+        beside = []
+        for one_j in range(j, j + JOIN):
+            side, p = one_j // half, one_j % half
+            one = right[p * rows : (p + 1) * rows, side * LANES : (side + 1) * LANES]
+            beside.append(jnp.concatenate([jnp.where(m, one, zero) for m in masks], axis=0))
+        product = dot(left, jnp.concatenate(beside, axis=1)).astype(BF16)
+        for n in range(JOIN):
+            for g in range(groups):
+                x_mat[(j + n) * residues : (j + n + 1) * residues, g * LANES : (g + 1) * LANES] = product[
+                    g * residues : (g + 1) * residues, n * LANES : (n + 1) * LANES
+                ]
+    coupling = coupling_ref[...]
+    projected = jnp.concatenate(
+        [
+            dot(x_mat[at : at + CHUNK, :], coupling) for at in range(0, residues * residues, CHUNK)
+        ], axis=0,
+    )
     counts = dot(dot(order, valid).astype(BF16), valid, ((1,), (1,)))
     counts = jnp.concatenate([counts, jnp.zeros((residues, LANES - residues), F32)], axis=1)
     for j in range(residues):
@@ -175,24 +192,28 @@
         yield at
 
 
-def transition_head(x_ref, *refs):
+def transition_part(start, x_ref, *refs):
     *weight_refs, out_ref = refs
-    for _ in transition_rows(x_ref, 0, out_ref.shape[0], *weight_refs, out_ref):
+    for _ in transition_rows(x_ref, start, out_ref.shape[0], *weight_refs, out_ref):
         pass
 
 
-def transition_tail(x_ref, *refs):
-    *weight_refs, head_ref, out_hbm, result_ref, sent = refs
-    head = head_ref.shape[0]
-    copies = [pltpu.make_async_copy(head_ref, out_hbm.at[pl.ds(0, head)], sent.at[0])]
-    copies[0].start()
+def transition_last(n_parts, x_ref, *refs):
+    weight_refs = refs[: -3 - n_parts]
+    part_refs = refs[-3 - n_parts : -3]
+    out_hbm, result_ref, sent = refs[-3:]
+    copies = []
+
+    def send(source, at, count):
+        copies.append(pltpu.make_async_copy(source, out_hbm.at[pl.ds(at, count)], sent.at[len(copies)]))
+        copies[-1].start()
+
+    head = 0
+    for part_ref in part_refs:
+        send(part_ref, head, part_ref.shape[0])
+        head += part_ref.shape[0]
     for at in transition_rows(x_ref, head, result_ref.shape[0], *weight_refs, result_ref):
-        copies.append(
-            pltpu.make_async_copy(
-                result_ref.at[pl.ds(at, STEP)], out_hbm.at[pl.ds(head + at, STEP)], sent.at[len(copies)]
-            )
-        )
-        copies[-1].start()
+        send(result_ref.at[pl.ds(at, STEP)], head + at, STEP)
     for copy in copies:
         copy.wait()
 
@@ -218,6 +239,11 @@
 
 def swap(array, size, apart):
     return lax.ppermute(array, "rows", [(i, i ^ apart) for i in range(size)])
+
+
+def hop(array, size, targets):
+    step = size // len(targets)
+    return lax.ppermute(array, "rows", [(i, targets[i // step] * step + i % step) for i in range(size)])
 
 
 def scatter_sum(partial, size):
@@ -240,37 +266,25 @@
     return pltpu.VMEM(shape, dtype)
 
 
-def transition(features, weights, head_rows):
+def transition(features, weights, start, count, parts=()):
     rows, residues, channels = features.shape
-    vmem = pl.BlockSpec(memory_space=pltpu.VMEM)
-    cost = lambda count: pl.CostEstimate(
-        flops=6_000_000 * count, bytes_accessed=30_000 * count, transcendentals=8_000 * count
-    )
-    params = pltpu.CompilerParams(vmem_limit_bytes=VMEM_LIMIT)
-    pinned = [pltpu.with_memory_space_constraint(a, pltpu.VMEM) for a in (features,) + tuple(weights)]
-    head = lambda: pl.pallas_call(
-        transition_head,
-        out_shape=inside((head_rows, residues, channels), BF16),
-        in_specs=[vmem] * len(pinned),
-        out_specs=vmem,
-        compiler_params=params,
-        cost_estimate=cost(head_rows),
-        name="transition_head",
-    )(*pinned)
-    tail = lambda before: pl.pallas_call(
-        transition_tail,
-        out_shape=jax.ShapeDtypeStruct(features.shape, BF16),
-        in_specs=[vmem] * (len(pinned) + 1),
-        out_specs=pl.BlockSpec(memory_space=pltpu.HBM),
+    operands = [features, *weights, *parts]
+    last = start + count == rows
+    return pl.pallas_call(
+        functools.partial(transition_last, len(parts)) if last else functools.partial(transition_part, start),
+        out_shape=jax.ShapeDtypeStruct(features.shape, BF16) if last else inside((count, residues, channels), BF16),
+        in_specs=[pl.BlockSpec(memory_space=pltpu.VMEM)] * len(operands),
+        out_specs=pl.BlockSpec(memory_space=pltpu.HBM if last else pltpu.VMEM),
         scratch_shapes=[
-            pltpu.VMEM((rows - head_rows, residues, channels), BF16),
-            pltpu.SemaphoreType.DMA((1 + (rows - head_rows) // STEP,)),
-        ],
-        compiler_params=params,
-        cost_estimate=cost(rows - head_rows),
-        name="transition_tail",
-    )(*pinned, pltpu.with_memory_space_constraint(before, pltpu.VMEM))
-    return head, tail
+            pltpu.VMEM((count, residues, channels), BF16),
+            pltpu.SemaphoreType.DMA((len(parts) + count // STEP,)),
+        ] if last else [],
+        compiler_params=pltpu.CompilerParams(vmem_limit_bytes=VMEM_LIMIT),
+        cost_estimate=pl.CostEstimate(
+            flops=6_000_000 * count, bytes_accessed=30_000 * count, transcendentals=8_000 * count
+        ),
+        name="transition_last" if last else "transition_part",
+    )(*(pltpu.with_memory_space_constraint(a, pltpu.VMEM) for a in operands))
 
 
 def body(
@@ -334,21 +348,23 @@
         compiler_params=pltpu.CompilerParams(vmem_limit_bytes=VMEM_LIMIT),
         name="outer_products",
     )(*(pltpu.with_memory_space_constraint(operand, pltpu.HBM) for operand in operands))
-    head, tail = transition(features, weights, rows // 4)
     if relative:
         keep = keep.reshape(2, 4, own, pair_channels)
-        head_rows = head()
-        got, head_rows = lax.optimization_barrier((swap(send, size, 1), head_rows))
+        first = transition(features, weights, 0, rows // 4)
+        got, first = lax.optimization_barrier((swap(send, size, 1), first))
         got = got.reshape(2, 4, own, pair_channels)
         away = keep[1] + got[1]
-        far = swap(away[:2], size, 2)
-        near = swap(away[2:], size, 2)
+        far_away, features = lax.optimization_barrier((away[:2], features))
+        far = swap(far_away, size, 2)
+        second = transition(features, weights, rows // 4, rows // 4)
+        near_away, second = lax.optimization_barrier((away[2:], second))
+        near = swap(near_away, size, 2)
         here = keep[0] + got[0]
         upper = here[:2] + far
-        two, three = swap(upper[0], size, 8), swap(upper[1], size, 12)
+        two, three = hop(upper[0], size, FIRST_HOP), hop(upper[1], size, SECOND_HOP)
         lower = here[2:] + near
         one = swap(lower[1], size, 4)
-        refreshed = tail(head_rows)
+        refreshed = transition(features, weights, rows // 2, rows // 2, (first, second))
         summands = (two, three, one, lower[0])
         pair_mean_update = pl.pallas_call(
             functools.partial(finish_kernel, residues),
@@ -358,7 +374,7 @@
             name="finish",
         )(*(pltpu.with_memory_space_constraint(a, pltpu.VMEM) for a in summands + (offset,)))
     else:
-        refreshed = tail(head())
+        refreshed = transition(features, weights, 0, rows)
         grid = jnp.concatenate([keep.reshape(residues // 2, residues, pair_channels),
                                 send.reshape(residues // 2, residues, pair_channels)], axis=0)
         counted = lax.psum(grid[:, residues - 1, :residues], "rows").reshape(size, own)

time: 22.4 us -> 20.7 us (0.924)
  waiting for transfers between devices: 4.03 us -> 3.26 us
  starting transfers between devices: 8.59 us -> 8.17 us
  Pallas kernels: 8.8 us -> 8.39 us
    ppermute x6 -> x4, starting transfers between devices: 8.59 us -> 4.13 us  [swap(): return lax.ppermute(array, 'rows', [(i, i ^ apart) for i in range(size)])]
    ppermute x0 -> x2, starting transfers between devices: none -> 4.04 us  [hop(): lax.ppermute(array, 'rows', [(i, targets[i // step] * step + i % step) fo...]
    ppermute x6 -> x4, waiting for transfers between devices: 4.03 us -> 2.21 us  [swap(): return lax.ppermute(array, 'rows', [(i, i ^ apart) for i in range(size)])]
    ppermute x0 -> x2, waiting for transfers between devices: none -> 1.05 us  [hop(): lax.ppermute(array, 'rows', [(i, targets[i // step] * step + i % step) fo...]
    pallas_call x1, Pallas kernels: 4.61 us -> 3.96 us  [body(): pl.pallas_call(functools.partial(outer_kernel, relative, len(operands), l...]
    pallas_call x2 -> x3, Pallas kernels: 3.47 us -> 3.71 us  [transition(): pl.pallas_call(functools.partial(transition_last, len(parts)) if last els...]
  transfers between devices with their start and end apart: 6 -> 6, of which waited for: 3 -> 4; matrix products, arithmetic and copies ran while one was open for 0% -> 0% of each run, Pallas kernels for 16% -> 18%
where the time goes in v3:
time: 20.7 us; the launch traced here: 20.6 us
  Pallas kernels  8.39 us (41%)
  starting transfers between devices  8.17 us (39%)
  waiting for transfers between devices  3.26 us (16%)
  between operations  0.7 us (3%)
    ppermute x4, starting transfers between devices, swap(): return lax.ppermute(array, 'rows', [(i, i ^ apart) for i in range(size)])  4.13 us
    ppermute x2, starting transfers between devices, hop(): lax.ppermute(array, 'rows', [(i, targets[i // step] * step + i % step) fo...  4.04 us
    pallas_call x1, Pallas kernels, body(): pl.pallas_call(functools.partial(outer_kernel, relative, len(operands), l...  3.96 us
    pallas_call x3, Pallas kernels, transition(): pl.pallas_call(functools.partial(transition_last, len(parts)) if last els...  3.71 us
    ppermute x4, waiting for transfers between devices, swap(): return lax.ppermute(array, 'rows', [(i, i ^ apart) for i in range(size)])  2.21 us
    ppermute x2, waiting for transfers between devices, hop(): lax.ppermute(array, 'rows', [(i, targets[i // step] * step + i % step) fo...  1.05 us
    pallas_call x1, Pallas kernels, body(): pl.pallas_call(functools.partial(finish_kernel, residues), out_shape=jax....  0.71 us
  transfers between devices with their start and end apart: 6, of which 4 were waited for; matrix products, arithmetic and copies ran while one was open for 0% of the time, Pallas kernels for 18%

profile of v3, /device:TPU:0, one launch (start us, length us, event | category | flops | bytes accessed | tf_op | source)
XLA Modules:
  0.0 20.6 jit_solution(6286531208212546288)
XLA Ops:
  0.6 4.0 %outer_products.1 = (f32[512,128]{1,0:T(8,128)S(1)}, f32[512,128]{1,0:T(8,128)S(1)}, bf16[64,32,64]{2,1,0:T(8,128)(2,1)S(1)}, f32[1,128]{1,0:T(1,128)S(1)}, f32[...) custom-call(bf16[64,32,64]{2,1,0:T(8,128)(2,1)} %refs_0_.1, ...), custom_call_target="tpu_custom_call" | custom-call | tf_op jit(solution)/shard_map/outer_products/pallas_call | solution.py:336
  4.6 0.5 %collective-permute-start = (f32[512,128]{1,0:T(8,128)S(1)}, f32[512,128]{1,0:T(8,128)S(1)}, u32[]{:S(2)}, u32[]{:S(2)}) collective-permute-start(f32[512,128]{1,0:T(8,128)S(1)} %get-tuple-element.18), channel_id=1, source_target_pairs={{0,1},{1,0},{2,3},{3,2},{4,5},{5,4},{6,7},{7,6},{8,9},{9,8},{10,11... | collective-permute-start | bytes 786440 | tf_op jit(solution)/shard_map/ppermute | solution.py:241
  5.1 0.8 %transition_part.2.refs_5_ = bf16[16,32,64]{2,1,0:T(8,128)(2,1)S(1)} custom-call(bf16[64,32,64]{2,1,0:T(8,128)(2,1)S(1)} %get-tuple-element.27.x_ref, f32[1,64]{1,0:T(1,128)S(1)} %get-tuple-element.20.refs_0_, f32[1,64]{1,0:T(1,128)S(1)} %get-tuple-element.21.refs_1_, bf16[64,256]{1,0:T(8,128)(2,1)S(1)} %get-tuple-element.22.refs_2_, ...), custom_call_target="tpu_custom_call" | custom-call | flops 96000000 | bytes 480000 | tf_op jit(solution)/shard_map/transition_part/pallas_call | solution.py:273
  5.9 0.3 %collective-permute-done = f32[512,128]{1,0:T(8,128)S(1)} collective-permute-done((f32[512,128]{1,0:T(8,128)S(1)}, f32[512,128]{1,0:T(8,128)S(1)}, u32[]{:S(2)}, u32[]{:S(2)}) %collective-permute-start) | collective-permute-done | bytes 262176 | tf_op jit(solution)/shard_map/ppermute | solution.py:241
  6.4 3.0 %collective-permute-start.1 = (f32[2,64,128]{2,1,0:T(8,128)S(1)}, f32[2,64,128]{2,1,0:T(8,128)S(1)}, u32[]{:S(2)}, u32[]{:S(2)}) collective-permute-start(f32[2,64,128]{2,1,0:T(8,128)S(1)} %bitcast.25), channel_id=1, source_target_pairs={{0,2},{1,3},{2,0},{3,1},{4,6},{5,7},{6,4},{7,5},{8,10},{9,11},{10,... | collective-permute-start | bytes 196616 | tf_op jit(solution)/shard_map/ppermute | solution.py:241
  9.3 0.8 %transition_part.3.refs_6_ = bf16[16,32,64]{2,1,0:T(8,128)(2,1)S(1)} custom-call(bf16[64,32,64]{2,1,0:T(8,128)(2,1)S(1)} %get-tuple-element.27.x_ref, f32[1,64]{1,0:T(1,128)S(1)} %get-tuple-element.20.refs_0_, f32[1,64]{1,0:T(1,128)S(1)} %get-tuple-element.21.refs_1_, bf16[64,256]{1,0:T(8,128)(2,1)S(1)} %get-tuple-element.22.refs_2_, ...), custom_call_target="tpu_custom_call" | custom-call | flops 96000000 | bytes 480000 | tf_op jit(solution)/shard_map/transition_part/pallas_call | solution.py:273
  10.1 0.1 collective-permute-start.4
  10.2 1.5 %collective-permute-done.1 = f32[2,64,128]{2,1,0:T(8,128)S(1)} collective-permute-done((f32[2,64,128]{2,1,0:T(8,128)S(1)}, f32[2,64,128]{2,1,0:T(8,128)S(1)}, u32[]{:S(2)}, u32[]{:S(2)}) %collective-permute-start.1) | collective-permute-done | bytes 65568 | tf_op jit(solution)/shard_map/ppermute | solution.py:241
  11.8 3.0 %collective-permute-start.2 = (f32[64,128]{1,0:T(8,128)S(1)}, f32[64,128]{1,0:T(8,128)S(1)}, u32[]{:S(2)}, u32[]{:S(2)}) collective-permute-start(f32[64,128]{1,0:T(8,128)S(1)} %get-tuple-element.41), channel_id=1, source_target_pairs={{0,8},{1,9},{2,10},{3,11},{4,12},{5,13},{6,14},{7,15},{8,4},{9,5},... | collective-permute-start | bytes 98312 | tf_op jit(solution)/shard_map/ppermute | solution.py:246
  14.7 1.1 %collective-permute-start.3 = (f32[64,128]{1,0:T(8,128)S(1)}, f32[64,128]{1,0:T(8,128)S(1)}, u32[]{:S(2)}, u32[]{:S(2)}) collective-permute-start(f32[64,128]{1,0:T(8,128)S(1)} %get-tuple-element.40), channel_id=1, source_target_pairs={{0,12},{1,13},{2,14},{3,15},{4,8},{5,9},{6,10},{7,11},{8,0},{9,1},... | collective-permute-start | bytes 98312 | tf_op jit(solution)/shard_map/ppermute | solution.py:246
  15.8 0.0 collective-permute-done.4
  15.8 0.6 %collective-permute-start.5 = (f32[64,128]{1,0:T(8,128)S(1)}, f32[64,128]{1,0:T(8,128)S(1)}, u32[]{:S(2)}, u32[]{:S(2)}) collective-permute-start(f32[64,128]{1,0:T(8,128)S(1)} %get-tuple-element.39), channel_id=1, source_target_pairs={{0,4},{1,5},{2,6},{3,7},{4,0},{5,1},{6,2},{7,3},{8,12},{9,13},{10,... | collective-permute-start | bytes 98312 | tf_op jit(solution)/shard_map/ppermute | solution.py:241
  16.4 2.1 %transition_last.1 = bf16[64,32,64]{2,1,0:T(8,128)(2,1)} custom-call(bf16[64,32,64]{2,1,0:T(8,128)(2,1)S(1)} %get-tuple-element.27.x_ref, f32[1,64]{1,0:T(1,128)S(1)} %get-tuple-element.20.refs_0_, f32[1,64]{1,0:T(1,128)S(1)} %get-tuple-element.21.refs_1_, bf16[64,256]{1,0:T(8,128)(2,1)S(1)} %get-tuple-element.22.refs_2_, ...), custom_call_target="tpu_custom_call" | custom-call | flops 192000000 | bytes 960000 | tf_op jit(solution)/shard_map/transition_last/pallas_call | solution.py:273
  18.5 0.0 collective-permute-done.2.refs_0_
  18.5 1.0 %collective-permute-done.3.refs_1_ = f32[64,128]{1,0:T(8,128)S(1)} collective-permute-done((f32[64,128]{1,0:T(8,128)S(1)}, f32[64,128]{1,0:T(8,128)S(1)}, u32[]{:S(2)}, u32[]{:S(2)}) %collective-permute-start.3) | collective-permute-done | bytes 32800 | tf_op jit(solution)/shard_map/ppermute | solution.py:246
  19.5 0.3 %collective-permute-done.5.refs_2_ = f32[64,128]{1,0:T(8,128)S(1)} collective-permute-done((f32[64,128]{1,0:T(8,128)S(1)}, f32[64,128]{1,0:T(8,128)S(1)}, u32[]{:S(2)}, u32[]{:S(2)}) %collective-permute-start.5) | collective-permute-done | bytes 32800 | tf_op jit(solution)/shard_map/ppermute | solution.py:241
  19.9 0.7 %finish.1 = f32[64,128]{1,0:T(8,128)} custom-call(f32[64,128]{1,0:T(8,128)S(1)} %collective-permute-done.2.refs_0_, f32[64,128]{1,0:T(8,128)S(1)} %collective-permute-done.3.refs_1_, f32[64,128]{1,0:T(8,128)S(1)} %collective-permute-done.5.refs_2_, f32[64,128]{1,0:T(8,128)S(1)} %get-tuple-element.38.refs_3_, f32[1,128]{1,0:T(1,128)S(1)} %get-tuple-element.29.refs_4_), custom_call_target="tpu_custom_call" | custom-call | tf_op jit(solution)/shard_map/finish/pallas_call | solution.py:369
  (6 shorter events, 0.1 us)
Async XLA Ops:
  4.6 1.7 %collective-permute-start = (f32[512,128]{1,0:T(8,128)S(1)}, f32[512,128]{1,0:T(8,128)S(1)}, u32[]{:S(2)}, u32[]{:S(2)}) collective-permute-start(f32[512,128]{1,0:T(8,128)S(1)} %get-tuple-element.18), channel_id=1, source_target_pairs={{0,1},{1,0},{2,3},{3,2},{4,5},{5,4},{6,7},{7,6},{8,9},{9,8},{10,11... | collective-permute-start | bytes 786440 | tf_op jit(solution)/shard_map/ppermute | solution.py:241
  6.4 5.4 %collective-permute-start.1 = (f32[2,64,128]{2,1,0:T(8,128)S(1)}, f32[2,64,128]{2,1,0:T(8,128)S(1)}, u32[]{:S(2)}, u32[]{:S(2)}) collective-permute-start(f32[2,64,128]{2,1,0:T(8,128)S(1)} %bitcast.25), channel_id=1, source_target_pairs={{0,2},{1,3},{2,0},{3,1},{4,6},{5,7},{6,4},{7,5},{8,10},{9,11},{10,... | collective-permute-start | bytes 196616 | tf_op jit(solution)/shard_map/ppermute | solution.py:241
  10.1 5.7 %collective-permute-start.4 = (f32[2,64,128]{2,1,0:T(8,128)S(1)}, f32[2,64,128]{2,1,0:T(8,128)S(1)}, u32[]{:S(2)}, u32[]{:S(2)}) collective-permute-start(f32[2,64,128]{2,1,0:T(8,128)S(1)} %bitcast.24), channel_id=1, source_target_pairs={{0,2},{1,3},{2,0},{3,1},{4,6},{5,7},{6,4},{7,5},{8,10},{9,11},{10,... | collective-permute-start | bytes 196616 | tf_op jit(solution)/shard_map/ppermute | solution.py:241
  11.8 6.7 %collective-permute-start.2 = (f32[64,128]{1,0:T(8,128)S(1)}, f32[64,128]{1,0:T(8,128)S(1)}, u32[]{:S(2)}, u32[]{:S(2)}) collective-permute-start(f32[64,128]{1,0:T(8,128)S(1)} %get-tuple-element.41), channel_id=1, source_target_pairs={{0,8},{1,9},{2,10},{3,11},{4,12},{5,13},{6,14},{7,15},{8,4},{9,5},... | collective-permute-start | bytes 98312 | tf_op jit(solution)/shard_map/ppermute | solution.py:246
  14.7 4.8 %collective-permute-start.3 = (f32[64,128]{1,0:T(8,128)S(1)}, f32[64,128]{1,0:T(8,128)S(1)}, u32[]{:S(2)}, u32[]{:S(2)}) collective-permute-start(f32[64,128]{1,0:T(8,128)S(1)} %get-tuple-element.40), channel_id=1, source_target_pairs={{0,12},{1,13},{2,14},{3,15},{4,8},{5,9},{6,10},{7,11},{8,0},{9,1},... | collective-permute-start | bytes 98312 | tf_op jit(solution)/shard_map/ppermute | solution.py:246
  15.8 4.1 %collective-permute-start.5 = (f32[64,128]{1,0:T(8,128)S(1)}, f32[64,128]{1,0:T(8,128)S(1)}, u32[]{:S(2)}, u32[]{:S(2)}) collective-permute-start(f32[64,128]{1,0:T(8,128)S(1)} %get-tuple-element.39), channel_id=1, source_target_pairs={{0,4},{1,5},{2,6},{3,7},{4,0},{5,1},{6,2},{7,3},{8,12},{9,13},{10,... | collective-permute-start | bytes 98312 | tf_op jit(solution)/shard_map/ppermute | solution.py:241

commit v4 on v3

--- a/solution.py
+++ b/solution.py
@@ -17,6 +17,9 @@
 CHUNK = 512
 FIRST_HOP = (2, 3, 1, 0)
 SECOND_HOP = (3, 2, 0, 1)
+LAST_HOP = (1, 0, 3, 2)
+TURNED = 0b0001
+UNLIKE = 1
 OWNERS = 16
 
 
@@ -55,32 +58,86 @@
     return centered * lax.rsqrt(variance + EPS) * gain + bias
 
 
+def ranks_along_z():
+    table = 0
+    for z, order in enumerate(zip(FIRST_HOP, SECOND_HOP, range(len(FIRST_HOP)), LAST_HOP)):
+        for place_of, other in enumerate(order):
+            table |= place_of << (z * 8 + (z ^ other) * 2)
+    return table - (1 << 32) if table >> 31 else table
+
+
+RANKS = ranks_along_z()
+
+
+def relabel(device):
+    return device ^ ((TURNED >> (device >> 2)) & 1)
+
+
 def place(residue, me, per_owner):
     if me is None:
         return residue
-    apart = (residue // per_owner) ^ me
-    along = apart >> 2
-    swapped = (along >> 1) & (me >> 3)
-    rank = (apart & 1) * 8 + ((apart >> 1) & 1) * 4 + ((along ^ 2) ^ swapped)
+    apart = relabel(residue // per_owner) ^ relabel(me)
+    along_y = (apart >> 1) & 1
+    along_z = (RANKS >> ((me >> 2) * 8 + (apart >> 2) * 2)) & 3
+    rank = (((apart & 1) ^ (along_y & UNLIKE)) * 2 + along_y) * 4 + along_z
     return rank * per_owner + residue % per_owner
+
+
+def outer_half(left, right, coupling, counts, x_mat, *out_refs):
+    count = counts.shape[0]
+    part = count // len(out_refs)
+    residues = out_refs[0].shape[0] // part
+    half = residues // 2
+    groups = left.shape[0] // count
+    rows = right.shape[0] // half
+    quad = left.shape[1] // rows
+    lane_group = iota((rows, LANES), 1) // (LANES // quad)
+    masks = [lane_group == h4 for h4 in range(quad)]
+    zero = jnp.zeros((rows, LANES), BF16)
+    for j in range(0, residues, JOIN):
+        beside = []
+        for one_j in range(j, j + JOIN):
+            side, p = one_j // half, one_j % half
+            one = right[p * rows : (p + 1) * rows, side * LANES : (side + 1) * LANES]
+            beside.append(jnp.concatenate([jnp.where(m, one, zero) for m in masks], axis=0))
+        product = dot(left, jnp.concatenate(beside, axis=1)).astype(BF16)
+        for n in range(JOIN):
+            for g in range(groups):
+                x_mat[(j + n) * count : (j + n + 1) * count, g * LANES : (g + 1) * LANES] = product[
+                    g * count : (g + 1) * count, n * LANES : (n + 1) * LANES
+                ]
+    projected = [
+        dot(x_mat[at : at + CHUNK, :], coupling) for at in range(0, residues * count, CHUNK)
+    ]
+    projected = jnp.concatenate(projected, axis=0)
+    for j in range(residues):
+        rows_j = counts if j == residues - 1 else projected[j * count : (j + 1) * count, :]
+        for n, out_ref in enumerate(out_refs):
+            out_ref[pl.ds(j, part, stride=residues), :] = rows_j[n * part : (n + 1) * part]
+
+
+def outer_second_kernel(left_ref, right_ref, coupling_ref, counts_ref, here_ref, away_ref, x_mat):
+    outer_half(left_ref[...], right_ref[...], coupling_ref[...], counts_ref[...], x_mat, here_ref, away_ref)
 
 
 def outer_kernel(relative, n_inputs, n_handed, *refs):
     sources = refs[:n_inputs]
-    keep_ref, send_ref = refs[n_inputs : n_inputs + 2]
-    handed = refs[n_inputs + 2 : n_inputs + 2 + n_handed]
+    outs, refs = refs[n_inputs : n_inputs + 5], refs[n_inputs + 5 :]
+    here_ref, away_ref, left_ref, right_ref, counts_ref = outs
+    handed = refs[:n_handed]
     own = n_inputs - n_handed
-    targets = refs[n_inputs + 2 + n_handed :][:own]
-    arrived, x_scratch, left_t_scratch, left_scratch, x_mat = refs[n_inputs + 2 + n_handed + own :]
-    presence_ref, position_ref, gain_ref, bias_ref, first_ref, second_ref, coupling_ref = targets
-    x_ref = handed[0]
+    early = own + 2
+    targets = refs[n_handed : n_handed + own]
+    arrived, x_scratch, left_t_scratch, left_scratch, x_mat = refs[n_handed + own :]
+    presence_ref, position_ref, gain_ref, bias_ref, first_ref, second_ref = targets
+    x_ref, coupling_ref = handed[:2]
     me = lax.axis_index("rows") if relative else None
     order = (handed[0],) + tuple(targets) + tuple(handed[1:])
     copies = [
         pltpu.make_async_copy(source, target, arrived.at[n])
         for n, (source, target) in enumerate(zip(sources, order))
     ]
-    for copy in copies[: own + 1]:
+    for copy in copies[:early]:
         copy.start()
     rows, residues, channels = x_ref.shape
     hidden = first_ref.shape[0]
@@ -97,9 +154,9 @@
     diagonal = iota(square, 0) == iota(square, 1)
     order = (place(iota(square, 1), me, per_owner) == iota(square, 0)).astype(BF16)
 
-    for copy in copies[own + 1 :]:
+    for copy in copies[early:]:
         copy.start()
-    for copy in copies[: own + 1]:
+    for copy in copies[:early]:
         copy.wait()
     x_scratch[...] = two_halves(x_ref[...], half).astype(F32).reshape(rows * half, 2 * channels)
     tokens = jnp.concatenate(
@@ -134,41 +191,21 @@
                         tile = jnp.where(low, turned[2 * c], pieces[2 * c + 1])
                     else:
                         tile = jnp.where(low, pieces[2 * c], turned[2 * c + 1])
-                    left_scratch[c, pl.ds(row, groups, stride=residues), :] = tile
+                    at = (row // half) * (groups * half) + row % half
+                    left_scratch[c, pl.ds(at, groups, stride=half), :] = tile
     left = jnp.concatenate(
         [left_scratch[c] for c in range(quad // 2)], axis=1
     ).astype(BF16)
 
     repeated = jnp.concatenate([second_ref[...]] * quad, axis=0)
     right = dot(normed, block_pair(repeated), ((1,), (1,))).astype(BF16)
-    lane_group = iota((rows, LANES), 1) // hidden
-    masks = [lane_group == h4 for h4 in range(quad)]
-    zero = jnp.zeros((rows, LANES), BF16)
-    for j in range(0, residues, JOIN):
-        beside = []
-        for one_j in range(j, j + JOIN):
-            side, p = one_j // half, one_j % half
-            one = right[p * rows : (p + 1) * rows, side * LANES : (side + 1) * LANES]
-            beside.append(jnp.concatenate([jnp.where(m, one, zero) for m in masks], axis=0))
-        product = dot(left, jnp.concatenate(beside, axis=1)).astype(BF16)
-        for n in range(JOIN):
-            for g in range(groups):
-                x_mat[(j + n) * residues : (j + n + 1) * residues, g * LANES : (g + 1) * LANES] = product[
-                    g * residues : (g + 1) * residues, n * LANES : (n + 1) * LANES
-                ]
-    coupling = coupling_ref[...]
-    projected = jnp.concatenate(
-        [
-            dot(x_mat[at : at + CHUNK, :], coupling) for at in range(0, residues * residues, CHUNK)
-        ], axis=0,
-    )
+    right_ref[...] = right
+    left_ref[...] = left[: groups * half]
     counts = dot(dot(order, valid).astype(BF16), valid, ((1,), (1,)))
     counts = jnp.concatenate([counts, jnp.zeros((residues, LANES - residues), F32)], axis=1)
-    for j in range(residues):
-        rows_j = counts if j == residues - 1 else projected[j * residues : (j + 1) * residues, :]
-        keep_ref[pl.ds(j, half, stride=residues), :] = rows_j[:half]
-        send_ref[pl.ds(j, half, stride=residues), :] = rows_j[half:]
-    for copy in copies[own + 1 :]:
+    counts_ref[...] = counts[:half]
+    outer_half(left[groups * half :], right, coupling_ref[...], counts[half:], x_mat, here_ref, away_ref)
+    for copy in copies[early:]:
         copy.wait()
 
 
@@ -243,7 +280,8 @@
 
 def hop(array, size, targets):
     step = size // len(targets)
-    return lax.ppermute(array, "rows", [(i, targets[i // step] * step + i % step) for i in range(size)])
+    pairs = [(i, relabel(targets[i // step] * step + relabel(i) % step)) for i in range(size)]
+    return lax.ppermute(array, "rows", pairs)
 
 
 def scatter_sum(partial, size):
@@ -319,10 +357,10 @@
         row(product_shift_vector),
         first_factor_matrix.T,
         second_factor_matrix.T,
-        coupling_matrix,
     )
     handed = (
         sequence_features,
+        coupling_matrix,
         row(coupling_offset),
         row(feedforward_scale_vector),
         row(feedforward_shift_vector),
@@ -331,9 +369,16 @@
         feedforward_contract_matrix.T,
     )
     operands = handed[:1] + used + handed[1:]
-    results = [inside((pairs // 2, pair_channels), F32)] * 2
+    split = (pairs * hidden // LANES // 2, rows * LANES // hidden)
+    results = [
+        inside((pairs // 4, pair_channels), F32),
+        inside((pairs // 4, pair_channels), F32),
+        inside(split, BF16),
+        inside((rows * residues // 2, 2 * LANES), BF16),
+        inside((residues // 2, LANES), F32),
+    ]
     results += [inside(operand.shape, operand.dtype) for operand in handed]
-    keep, send, features, offset, *weights = pl.pallas_call(
+    send_here, send_away, left, right, counts, features, coupling, offset, *weights = pl.pallas_call(
         functools.partial(outer_kernel, relative, len(operands), len(handed)),
         out_shape=results,
         in_specs=[pl.BlockSpec(memory_space=pltpu.HBM)] * len(operands),
@@ -343,29 +388,38 @@
             pltpu.VMEM((rows * residues // 2, 2 * channels), F32),
             pltpu.VMEM((rows * residues // 2 // LANES, 2 * hidden, LANES), F32),
             pltpu.VMEM((rows // hidden, pairs * hidden // LANES, LANES), F32),
-            pltpu.VMEM((pairs, hidden * hidden), BF16),
+            pltpu.VMEM((pairs // 2, hidden * hidden), BF16),
         ],
         compiler_params=pltpu.CompilerParams(vmem_limit_bytes=VMEM_LIMIT),
         name="outer_products",
     )(*(pltpu.with_memory_space_constraint(operand, pltpu.HBM) for operand in operands))
+    kept = (left, right, coupling, counts)
+    keep_here, keep_away = pl.pallas_call(
+        outer_second_kernel,
+        out_shape=[inside((pairs // 4, pair_channels), F32)] * 2,
+        in_specs=[pl.BlockSpec(memory_space=pltpu.VMEM)] * len(kept),
+        out_specs=[pl.BlockSpec(memory_space=pltpu.VMEM)] * 2,
+        scratch_shapes=[pltpu.VMEM((pairs // 2, hidden * hidden), BF16)],
+        compiler_params=pltpu.CompilerParams(vmem_limit_bytes=VMEM_LIMIT),
+        cost_estimate=pl.CostEstimate(flops=1_000_000_000, bytes_accessed=2_000_000, transcendentals=0),
+        name="outer_second",
+    )(*(pltpu.with_memory_space_constraint(a, pltpu.VMEM) for a in kept))
     if relative:
-        keep = keep.reshape(2, 4, own, pair_channels)
+        got_here = swap(send_here, size, 1)
+        got_away, keep_away = lax.optimization_barrier((swap(send_away, size, 1), keep_away))
+        away = (keep_away + got_away).reshape(4, own, pair_channels)
+        far_away, features = lax.optimization_barrier((away[:2], features))
+        far = swap(far_away, size, 2 + UNLIKE)
         first = transition(features, weights, 0, rows // 4)
-        got, first = lax.optimization_barrier((swap(send, size, 1), first))
-        got = got.reshape(2, 4, own, pair_channels)
-        away = keep[1] + got[1]
-        far_away, features = lax.optimization_barrier((away[:2], features))
-        far = swap(far_away, size, 2)
-        second = transition(features, weights, rows // 4, rows // 4)
-        near_away, second = lax.optimization_barrier((away[2:], second))
-        near = swap(near_away, size, 2)
-        here = keep[0] + got[0]
+        near_away, first = lax.optimization_barrier((away[2:], first))
+        near = swap(near_away, size, 2 + UNLIKE)
+        here = (keep_here + got_here).reshape(4, own, pair_channels)
         upper = here[:2] + far
         two, three = hop(upper[0], size, FIRST_HOP), hop(upper[1], size, SECOND_HOP)
         lower = here[2:] + near
-        one = swap(lower[1], size, 4)
-        refreshed = transition(features, weights, rows // 2, rows // 2, (first, second))
-        summands = (two, three, one, lower[0])
+        one = hop(lower[1], size, LAST_HOP)
+        refreshed = transition(features, weights, rows // 4, rows - rows // 4, (first,))
+        summands = (three, two, one, lower[0])
         pair_mean_update = pl.pallas_call(
             functools.partial(finish_kernel, residues),
             out_shape=jax.ShapeDtypeStruct((own, pair_channels), F32),
@@ -375,8 +429,8 @@
         )(*(pltpu.with_memory_space_constraint(a, pltpu.VMEM) for a in summands + (offset,)))
     else:
         refreshed = transition(features, weights, 0, rows)
-        grid = jnp.concatenate([keep.reshape(residues // 2, residues, pair_channels),
-                                send.reshape(residues // 2, residues, pair_channels)], axis=0)
+        grid = jnp.concatenate([keep_here, keep_away, send_here, send_away], axis=0)
+        grid = grid.reshape(residues, residues, pair_channels)
         counted = lax.psum(grid[:, residues - 1, :residues], "rows").reshape(size, own)
         counted = pick(counted, lax.axis_index("rows"), 0)[:, None]
         last = iota(grid.shape, 1) == residues - 1

time: 20.7 us -> 19.5 us (0.942)
  waiting for transfers between devices: 3.26 us -> 2.11 us
  starting transfers between devices: 8.17 us -> 7.75 us
  Pallas kernels: 8.39 us -> 8.72 us
    ppermute x4, waiting for transfers between devices: 2.21 us -> 1.33 us  [swap(): return lax.ppermute(array, 'rows', [(i, i ^ apart) for i in range(size)])]
    pallas_call x0 -> x1, Pallas kernels: none -> 0.87 us  [body(): pl.pallas_call(outer_second_kernel, out_shape=[inside((pairs // 4, pair_c...]
    ppermute x4, starting transfers between devices: 4.13 us -> 3.6 us  [swap(): return lax.ppermute(array, 'rows', [(i, i ^ apart) for i in range(size)])]
    pallas_call x1, Pallas kernels: 3.96 us -> 3.64 us  [body(): pl.pallas_call(functools.partial(outer_kernel, relative, len(operands), l...]
    ppermute x2 -> x3, waiting for transfers between devices: 1.05 us -> 0.78 us  [hop(): return lax.ppermute(array, 'rows', pairs)]
    pallas_call x3 -> x2, Pallas kernels: 3.71 us -> 3.49 us  [transition(): pl.pallas_call(functools.partial(transition_last, len(parts)) if last els...]
    ppermute x2 -> x3, starting transfers between devices: 4.04 us -> 4.16 us  [hop(): return lax.ppermute(array, 'rows', pairs)]
  transfers between devices with their start and end apart: 6 -> 7, of which waited for: 4 -> 3; matrix products, arithmetic and copies ran while one was open for 0% -> 0% of each run, Pallas kernels for 18% -> 22%
where the time goes in v4:
time: 19.5 us; the launch traced here: 19.4 us
  Pallas kernels  8.72 us (45%)
  starting transfers between devices  7.75 us (40%)
  waiting for transfers between devices  2.11 us (11%)
  between operations  0.72 us (4%)
    ppermute x3, starting transfers between devices, hop(): return lax.ppermute(array, 'rows', pairs)  4.16 us
    pallas_call x1, Pallas kernels, body(): pl.pallas_call(functools.partial(outer_kernel, relative, len(operands), l...  3.64 us
    ppermute x4, starting transfers between devices, swap(): return lax.ppermute(array, 'rows', [(i, i ^ apart) for i in range(size)])  3.6 us
    pallas_call x2, Pallas kernels, transition(): pl.pallas_call(functools.partial(transition_last, len(parts)) if last els...  3.49 us
    ppermute x4, waiting for transfers between devices, swap(): return lax.ppermute(array, 'rows', [(i, i ^ apart) for i in range(size)])  1.33 us
    pallas_call x1, Pallas kernels, body(): pl.pallas_call(outer_second_kernel, out_shape=[inside((pairs // 4, pair_c...  0.87 us
    ppermute x3, waiting for transfers between devices, hop(): return lax.ppermute(array, 'rows', pairs)  0.78 us
    pallas_call x1, Pallas kernels, body(): pl.pallas_call(functools.partial(finish_kernel, residues), out_shape=jax....  0.71 us
  transfers between devices with their start and end apart: 7, of which 3 were waited for; matrix products, arithmetic and copies ran while one was open for 0% of the time, Pallas kernels for 22%

profile of v4, /device:TPU:0, one launch (start us, length us, event | category | flops | bytes accessed | tf_op | source)
XLA Modules:
  0.0 19.4 jit_solution(15650371384912671312)
XLA Ops:
  0.6 3.6 %outer_products.1 = (f32[256,128]{1,0:T(8,128)S(1)}, f32[256,128]{1,0:T(8,128)S(1)}, bf16[128,256]{1,0:T(8,128)(2,1)S(1)}, bf16[1024,256]{1,0:T(8,128)(2,1)S(1)}...) custom-call(bf16[64,32,64]{2,1,0:T(8,128)(2,1)} %refs_0_.1, ...), custom_call_target="tpu_custom_call" | custom-call | tf_op jit(solution)/shard_map/outer_products/pallas_call | solution.py:381
  4.3 0.5 %collective-permute-start.1 = (f32[256,128]{1,0:T(8,128)S(1)}, f32[256,128]{1,0:T(8,128)S(1)}, u32[]{:S(2)}, u32[]{:S(2)}) collective-permute-start(f32[256,128]{1,0:T(8,128)S(1)} %get-tuple-element.29), channel_id=1, source_target_pairs={{0,1},{1,0},{2,3},{3,2},{4,5},{5,4},{6,7},{7,6},{8,9},{9,8},{10,11... | collective-permute-start | bytes 393224 | tf_op jit(solution)/shard_map/ppermute | solution.py:278
  4.8 0.1 collective-permute-start
  4.9 0.9 %outer_second.1 = (f32[256,128]{1,0:T(8,128)S(1)}, f32[256,128]{1,0:T(8,128)S(1)}) custom-call(bf16[128,256]{1,0:T(8,128)(2,1)S(1)} %get-tuple-element.23.left_ref, bf16[1024,256]{1,0:T(8,128)(2,1)S(1)} %get-tuple-element.24.right_ref, bf16[1024,128]{1,0:T(8,128)(2,1)S(1)} %get-tuple-element.25.coupling_ref, f32[16,128]{1,0:T(8,128)S(1)} %get-tuple-element.26.counts_ref), custom_call_target="tpu_custom_call" | custom-call | flops 1000000000 | bytes 2000000 | tf_op jit(solution)/shard_map/outer_second/pallas_call | solution.py:397
  5.8 0.0 collective-permute-done.1
  5.8 2.7 %collective-permute-start.2 = (f32[2,64,128]{2,1,0:T(8,128)S(1)}, f32[2,64,128]{2,1,0:T(8,128)S(1)}, u32[]{:S(2)}, u32[]{:S(2)}) collective-permute-start(f32[2,64,128]{2,1,0:T(8,128)S(1)} %bitcast.25), channel_id=1, source_target_pairs={{0,3},{1,2},{2,1},{3,0},{4,7},{5,6},{6,5},{7,4},{8,11},{9,10},{10,... | collective-permute-start | bytes 196616 | tf_op jit(solution)/shard_map/ppermute | solution.py:278
  8.5 0.0 collective-permute-done
  8.6 0.8 %transition_part.1.refs_5_ = bf16[16,32,64]{2,1,0:T(8,128)(2,1)S(1)} custom-call(bf16[64,32,64]{2,1,0:T(8,128)(2,1)S(1)} %get-tuple-element.35.x_ref, f32[1,64]{1,0:T(1,128)S(1)} %get-tuple-element.36.refs_0_, f32[1,64]{1,0:T(1,128)S(1)} %get-tuple-element.37.refs_1_, bf16[64,256]{1,0:T(8,128)(2,1)S(1)} %get-tuple-element.38.refs_2_, ...), custom_call_target="tpu_custom_call" | custom-call | flops 96000000 | bytes 480000 | tf_op jit(solution)/shard_map/transition_part/pallas_call | solution.py:311
  9.4 0.3 %collective-permute-start.5 = (f32[2,64,128]{2,1,0:T(8,128)S(1)}, f32[2,64,128]{2,1,0:T(8,128)S(1)}, u32[]{:S(2)}, u32[]{:S(2)}) collective-permute-start(f32[2,64,128]{2,1,0:T(8,128)S(1)} %bitcast.24), channel_id=1, source_target_pairs={{0,3},{1,2},{2,1},{3,0},{4,7},{5,6},{6,5},{7,4},{8,11},{9,10},{10,... | collective-permute-start | bytes 196616 | tf_op jit(solution)/shard_map/ppermute | solution.py:278
  9.7 1.3 %collective-permute-done.2 = f32[2,64,128]{2,1,0:T(8,128)S(1)} collective-permute-done((f32[2,64,128]{2,1,0:T(8,128)S(1)}, f32[2,64,128]{2,1,0:T(8,128)S(1)}, u32[]{:S(2)}, u32[]{:S(2)}) %collective-permute-start.2) | collective-permute-done | bytes 65568 | tf_op jit(solution)/shard_map/ppermute | solution.py:278
  11.0 2.8 %collective-permute-start.4 = (f32[64,128]{1,0:T(8,128)S(1)}, f32[64,128]{1,0:T(8,128)S(1)}, u32[]{:S(2)}, u32[]{:S(2)}) collective-permute-start(f32[64,128]{1,0:T(8,128)S(1)} %get-tuple-element.50), channel_id=1, source_target_pairs={{0,9},{1,8},{2,11},{3,10},{4,12},{5,13},{6,14},{7,15},{8,4},{9,5},... | collective-permute-start | bytes 98312 | tf_op jit(solution)/shard_map/ppermute | solution.py:284
  13.8 1.1 %collective-permute-start.3 = (f32[64,128]{1,0:T(8,128)S(1)}, f32[64,128]{1,0:T(8,128)S(1)}, u32[]{:S(2)}, u32[]{:S(2)}) collective-permute-start(f32[64,128]{1,0:T(8,128)S(1)} %get-tuple-element.51), channel_id=1, source_target_pairs={{0,13},{1,12},{2,15},{3,14},{4,8},{5,9},{6,10},{7,11},{8,1},{9,0},... | collective-permute-start | bytes 98312 | tf_op jit(solution)/shard_map/ppermute | solution.py:284
  14.9 0.0 collective-permute-done.5
  14.9 0.3 %collective-permute-start.6 = (f32[64,128]{1,0:T(8,128)S(1)}, f32[64,128]{1,0:T(8,128)S(1)}, u32[]{:S(2)}, u32[]{:S(2)}) collective-permute-start(f32[64,128]{1,0:T(8,128)S(1)} %get-tuple-element.49), channel_id=1, source_target_pairs={{0,5},{1,4},{2,7},{3,6},{4,1},{5,0},{6,3},{7,2},{8,12},{9,13},{10,... | collective-permute-start | bytes 98312 | tf_op jit(solution)/shard_map/ppermute | solution.py:284
  15.2 2.7 %transition_last.1 = bf16[64,32,64]{2,1,0:T(8,128)(2,1)} custom-call(bf16[64,32,64]{2,1,0:T(8,128)(2,1)S(1)} %get-tuple-element.35.x_ref, f32[1,64]{1,0:T(1,128)S(1)} %get-tuple-element.36.refs_0_, f32[1,64]{1,0:T(1,128)S(1)} %get-tuple-element.37.refs_1_, bf16[64,256]{1,0:T(8,128)(2,1)S(1)} %get-tuple-element.38.refs_2_, ...), custom_call_target="tpu_custom_call" | custom-call | flops 288000000 | bytes 1440000 | tf_op jit(solution)/shard_map/transition_last/pallas_call | solution.py:311
  17.9 0.0 collective-permute-done.4.refs_1_
  17.9 0.2 collective-permute-done.3.refs_0_
  18.1 0.6 %collective-permute-done.6.refs_2_ = f32[64,128]{1,0:T(8,128)S(1)} collective-permute-done((f32[64,128]{1,0:T(8,128)S(1)}, f32[64,128]{1,0:T(8,128)S(1)}, u32[]{:S(2)}, u32[]{:S(2)}) %collective-permute-start.6) | collective-permute-done | bytes 32800 | tf_op jit(solution)/shard_map/ppermute | solution.py:284
  18.7 0.7 %finish.1 = f32[64,128]{1,0:T(8,128)} custom-call(f32[64,128]{1,0:T(8,128)S(1)} %collective-permute-done.3.refs_0_, f32[64,128]{1,0:T(8,128)S(1)} %collective-permute-done.4.refs_1_, f32[64,128]{1,0:T(8,128)S(1)} %collective-permute-done.6.refs_2_, f32[64,128]{1,0:T(8,128)S(1)} %get-tuple-element.48.refs_3_, f32[1,128]{1,0:T(1,128)S(1)} %get-tuple-element.42.refs_4_), custom_call_target="tpu_custom_call" | custom-call | tf_op jit(solution)/shard_map/finish/pallas_call | solution.py:423
  (8 shorter events, 0.1 us)
Async XLA Ops:
  4.3 1.5 %collective-permute-start.1 = (f32[256,128]{1,0:T(8,128)S(1)}, f32[256,128]{1,0:T(8,128)S(1)}, u32[]{:S(2)}, u32[]{:S(2)}) collective-permute-start(f32[256,128]{1,0:T(8,128)S(1)} %get-tuple-element.29), channel_id=1, source_target_pairs={{0,1},{1,0},{2,3},{3,2},{4,5},{5,4},{6,7},{7,6},{8,9},{9,8},{10,11... | collective-permute-start | bytes 393224 | tf_op jit(solution)/shard_map/ppermute | solution.py:278
  4.8 3.7 %collective-permute-start = (f32[256,128]{1,0:T(8,128)S(1)}, f32[256,128]{1,0:T(8,128)S(1)}, u32[]{:S(2)}, u32[]{:S(2)}) collective-permute-start(f32[256,128]{1,0:T(8,128)S(1)} %get-tuple-element.28), channel_id=1, source_target_pairs={{0,1},{1,0},{2,3},{3,2},{4,5},{5,4},{6,7},{7,6},{8,9},{9,8},{10,11... | collective-permute-start | bytes 393224 | tf_op jit(solution)/shard_map/ppermute | solution.py:278
  5.8 5.2 %collective-permute-start.2 = (f32[2,64,128]{2,1,0:T(8,128)S(1)}, f32[2,64,128]{2,1,0:T(8,128)S(1)}, u32[]{:S(2)}, u32[]{:S(2)}) collective-permute-start(f32[2,64,128]{2,1,0:T(8,128)S(1)} %bitcast.25), channel_id=1, source_target_pairs={{0,3},{1,2},{2,1},{3,0},{4,7},{5,6},{6,5},{7,4},{8,11},{9,10},{10,... | collective-permute-start | bytes 196616 | tf_op jit(solution)/shard_map/ppermute | solution.py:278
  9.4 5.5 %collective-permute-start.5 = (f32[2,64,128]{2,1,0:T(8,128)S(1)}, f32[2,64,128]{2,1,0:T(8,128)S(1)}, u32[]{:S(2)}, u32[]{:S(2)}) collective-permute-start(f32[2,64,128]{2,1,0:T(8,128)S(1)} %bitcast.24), channel_id=1, source_target_pairs={{0,3},{1,2},{2,1},{3,0},{4,7},{5,6},{6,5},{7,4},{8,11},{9,10},{10,... | collective-permute-start | bytes 196616 | tf_op jit(solution)/shard_map/ppermute | solution.py:278
  11.0 6.9 %collective-permute-start.4 = (f32[64,128]{1,0:T(8,128)S(1)}, f32[64,128]{1,0:T(8,128)S(1)}, u32[]{:S(2)}, u32[]{:S(2)}) collective-permute-start(f32[64,128]{1,0:T(8,128)S(1)} %get-tuple-element.50), channel_id=1, source_target_pairs={{0,9},{1,8},{2,11},{3,10},{4,12},{5,13},{6,14},{7,15},{8,4},{9,5},... | collective-permute-start | bytes 98312 | tf_op jit(solution)/shard_map/ppermute | solution.py:284
  13.8 4.2 %collective-permute-start.3 = (f32[64,128]{1,0:T(8,128)S(1)}, f32[64,128]{1,0:T(8,128)S(1)}, u32[]{:S(2)}, u32[]{:S(2)}) collective-permute-start(f32[64,128]{1,0:T(8,128)S(1)} %get-tuple-element.51), channel_id=1, source_target_pairs={{0,13},{1,12},{2,15},{3,14},{4,8},{5,9},{6,10},{7,11},{8,1},{9,0},... | collective-permute-start | bytes 98312 | tf_op jit(solution)/shard_map/ppermute | solution.py:284
  14.9 3.7 %collective-permute-start.6 = (f32[64,128]{1,0:T(8,128)S(1)}, f32[64,128]{1,0:T(8,128)S(1)}, u32[]{:S(2)}, u32[]{:S(2)}) collective-permute-start(f32[64,128]{1,0:T(8,128)S(1)} %get-tuple-element.49), channel_id=1, source_target_pairs={{0,5},{1,4},{2,7},{3,6},{4,1},{5,0},{6,3},{7,2},{8,12},{9,13},{10,... | collective-permute-start | bytes 98312 | tf_op jit(solution)/shard_map/ppermute | solution.py:284

commit v5 on v4

--- a/solution.py
+++ b/solution.py
@@ -14,7 +14,7 @@
 VMEM_LIMIT = 48 * 1024 * 1024
 STEP = 16
 JOIN = 2
-CHUNK = 512
+CHUNK = 256
 FIRST_HOP = (2, 3, 1, 0)
 SECOND_HOP = (3, 2, 0, 1)
 LAST_HOP = (1, 0, 3, 2)
@@ -410,7 +410,7 @@
         away = (keep_away + got_away).reshape(4, own, pair_channels)
         far_away, features = lax.optimization_barrier((away[:2], features))
         far = swap(far_away, size, 2 + UNLIKE)
-        first = transition(features, weights, 0, rows // 4)
+        first = transition(features, weights, 0, rows // 2)
         near_away, first = lax.optimization_barrier((away[2:], first))
         near = swap(near_away, size, 2 + UNLIKE)
         here = (keep_here + got_here).reshape(4, own, pair_channels)
@@ -418,7 +418,7 @@
         two, three = hop(upper[0], size, FIRST_HOP), hop(upper[1], size, SECOND_HOP)
         lower = here[2:] + near
         one = hop(lower[1], size, LAST_HOP)
-        refreshed = transition(features, weights, rows // 4, rows - rows // 4, (first,))
+        refreshed = transition(features, weights, rows // 2, rows - rows // 2, (first,))
         summands = (three, two, one, lower[0])
         pair_mean_update = pl.pallas_call(
             functools.partial(finish_kernel, residues),

time: 19.5 us -> 19.3 us (0.990)
  starting transfers between devices: 7.75 us -> 8.38 us
  Pallas kernels: 8.72 us -> 8.27 us
  waiting for transfers between devices: 2.11 us -> 1.67 us
    ppermute x4, waiting for transfers between devices: 1.33 us -> 0.5 us  [swap(): return lax.ppermute(array, 'rows', [(i, i ^ apart) for i in range(size)])]
    ppermute x3, starting transfers between devices: 4.16 us -> 4.78 us  [hop(): return lax.ppermute(array, 'rows', pairs)]
    ppermute x3, waiting for transfers between devices: 0.78 us -> 1.17 us  [hop(): return lax.ppermute(array, 'rows', pairs)]
    pallas_call x1, Pallas kernels: 3.64 us -> 3.27 us  [body(): pl.pallas_call(functools.partial(outer_kernel, relative, len(operands), l...]
  transfers between devices with their start and end apart: 7 -> 7, of which waited for: 3 -> 4; matrix products, arithmetic and copies ran while one was open for 0% -> 0% of each run, Pallas kernels for 22% -> 22%
where the time goes in v5:
time: 19.3 us; the launch traced here: 19.1 us
  starting transfers between devices  8.38 us (43%)
  Pallas kernels  8.27 us (43%)
  waiting for transfers between devices  1.67 us (9%)
  between operations  0.72 us (4%)
    ppermute x3, starting transfers between devices, hop(): return lax.ppermute(array, 'rows', pairs)  4.78 us
    ppermute x4, starting transfers between devices, swap(): return lax.ppermute(array, 'rows', [(i, i ^ apart) for i in range(size)])  3.6 us
    pallas_call x2, Pallas kernels, transition(): pl.pallas_call(functools.partial(transition_last, len(parts)) if last els...  3.46 us
    pallas_call x1, Pallas kernels, body(): pl.pallas_call(functools.partial(outer_kernel, relative, len(operands), l...  3.27 us
    ppermute x3, waiting for transfers between devices, hop(): return lax.ppermute(array, 'rows', pairs)  1.17 us
    pallas_call x1, Pallas kernels, body(): pl.pallas_call(outer_second_kernel, out_shape=[inside((pairs // 4, pair_c...  0.83 us
    pallas_call x1, Pallas kernels, body(): pl.pallas_call(functools.partial(finish_kernel, residues), out_shape=jax....  0.71 us
    ppermute x4, waiting for transfers between devices, swap(): return lax.ppermute(array, 'rows', [(i, i ^ apart) for i in range(size)])  0.5 us
  transfers between devices with their start and end apart: 7, of which 4 were waited for; matrix products, arithmetic and copies ran while one was open for 0% of the time, Pallas kernels for 22%

profile of v5, /device:TPU:0, one launch (start us, length us, event | category | flops | bytes accessed | tf_op | source)
XLA Modules:
  0.0 19.1 jit_solution(4938932193954204161)
XLA Ops:
  0.6 3.3 %outer_products.1 = (f32[256,128]{1,0:T(8,128)S(1)}, f32[256,128]{1,0:T(8,128)S(1)}, bf16[128,256]{1,0:T(8,128)(2,1)S(1)}, bf16[1024,256]{1,0:T(8,128)(2,1)S(1)}...) custom-call(bf16[64,32,64]{2,1,0:T(8,128)(2,1)} %refs_0_.1, ...), custom_call_target="tpu_custom_call" | custom-call | tf_op jit(solution)/shard_map/outer_products/pallas_call | solution.py:381
  3.9 0.5 %collective-permute-start.1 = (f32[256,128]{1,0:T(8,128)S(1)}, f32[256,128]{1,0:T(8,128)S(1)}, u32[]{:S(2)}, u32[]{:S(2)}) collective-permute-start(f32[256,128]{1,0:T(8,128)S(1)} %get-tuple-element.29), channel_id=1, source_target_pairs={{0,1},{1,0},{2,3},{3,2},{4,5},{5,4},{6,7},{7,6},{8,9},{9,8},{10,11... | collective-permute-start | bytes 393224 | tf_op jit(solution)/shard_map/ppermute | solution.py:278
  4.4 0.1 collective-permute-start
  4.5 0.8 %outer_second.1 = (f32[256,128]{1,0:T(8,128)S(1)}, f32[256,128]{1,0:T(8,128)S(1)}) custom-call(bf16[128,256]{1,0:T(8,128)(2,1)S(1)} %get-tuple-element.23.left_ref, bf16[1024,256]{1,0:T(8,128)(2,1)S(1)} %get-tuple-element.24.right_ref, bf16[1024,128]{1,0:T(8,128)(2,1)S(1)} %get-tuple-element.25.coupling_ref, f32[16,128]{1,0:T(8,128)S(1)} %get-tuple-element.26.counts_ref), custom_call_target="tpu_custom_call" | custom-call | flops 1000000000 | bytes 2000000 | tf_op jit(solution)/shard_map/outer_second/pallas_call | solution.py:397
  5.3 0.1 collective-permute-done.1
  5.5 2.7 %collective-permute-start.2 = (f32[2,64,128]{2,1,0:T(8,128)S(1)}, f32[2,64,128]{2,1,0:T(8,128)S(1)}, u32[]{:S(2)}, u32[]{:S(2)}) collective-permute-start(f32[2,64,128]{2,1,0:T(8,128)S(1)} %bitcast.25), channel_id=1, source_target_pairs={{0,3},{1,2},{2,1},{3,0},{4,7},{5,6},{6,5},{7,4},{8,11},{9,10},{10,... | collective-permute-start | bytes 196616 | tf_op jit(solution)/shard_map/ppermute | solution.py:278
  8.2 0.0 collective-permute-done
  8.2 1.4 %transition_part.1.refs_5_ = bf16[32,32,64]{2,1,0:T(8,128)(2,1)S(1)} custom-call(bf16[64,32,64]{2,1,0:T(8,128)(2,1)S(1)} %get-tuple-element.35.x_ref, f32[1,64]{1,0:T(1,128)S(1)} %get-tuple-element.36.refs_0_, f32[1,64]{1,0:T(1,128)S(1)} %get-tuple-element.37.refs_1_, bf16[64,256]{1,0:T(8,128)(2,1)S(1)} %get-tuple-element.38.refs_2_, ...), custom_call_target="tpu_custom_call" | custom-call | flops 192000000 | bytes 960000 | tf_op jit(solution)/shard_map/transition_part/pallas_call | solution.py:311
  9.6 0.3 %collective-permute-start.5 = (f32[2,64,128]{2,1,0:T(8,128)S(1)}, f32[2,64,128]{2,1,0:T(8,128)S(1)}, u32[]{:S(2)}, u32[]{:S(2)}) collective-permute-start(f32[2,64,128]{2,1,0:T(8,128)S(1)} %bitcast.24), channel_id=1, source_target_pairs={{0,3},{1,2},{2,1},{3,0},{4,7},{5,6},{6,5},{7,4},{8,11},{9,10},{10,... | collective-permute-start | bytes 196616 | tf_op jit(solution)/shard_map/ppermute | solution.py:278
  9.9 0.4 %collective-permute-done.2 = f32[2,64,128]{2,1,0:T(8,128)S(1)} collective-permute-done((f32[2,64,128]{2,1,0:T(8,128)S(1)}, f32[2,64,128]{2,1,0:T(8,128)S(1)}, u32[]{:S(2)}, u32[]{:S(2)}) %collective-permute-start.2) | collective-permute-done | bytes 65568 | tf_op jit(solution)/shard_map/ppermute | solution.py:278
  10.4 3.0 %collective-permute-start.4 = (f32[64,128]{1,0:T(8,128)S(1)}, f32[64,128]{1,0:T(8,128)S(1)}, u32[]{:S(2)}, u32[]{:S(2)}) collective-permute-start(f32[64,128]{1,0:T(8,128)S(1)} %get-tuple-element.50), channel_id=1, source_target_pairs={{0,9},{1,8},{2,11},{3,10},{4,12},{5,13},{6,14},{7,15},{8,4},{9,5},... | collective-permute-start | bytes 98312 | tf_op jit(solution)/shard_map/ppermute | solution.py:284
  13.4 1.1 %collective-permute-start.3 = (f32[64,128]{1,0:T(8,128)S(1)}, f32[64,128]{1,0:T(8,128)S(1)}, u32[]{:S(2)}, u32[]{:S(2)}) collective-permute-start(f32[64,128]{1,0:T(8,128)S(1)} %get-tuple-element.51), channel_id=1, source_target_pairs={{0,13},{1,12},{2,15},{3,14},{4,8},{5,9},{6,10},{7,11},{8,1},{9,0},... | collective-permute-start | bytes 98312 | tf_op jit(solution)/shard_map/ppermute | solution.py:284
  14.5 0.0 collective-permute-done.5
  14.5 0.7 %collective-permute-start.6 = (f32[64,128]{1,0:T(8,128)S(1)}, f32[64,128]{1,0:T(8,128)S(1)}, u32[]{:S(2)}, u32[]{:S(2)}) collective-permute-start(f32[64,128]{1,0:T(8,128)S(1)} %get-tuple-element.49), channel_id=1, source_target_pairs={{0,5},{1,4},{2,7},{3,6},{4,1},{5,0},{6,3},{7,2},{8,12},{9,13},{10,... | collective-permute-start | bytes 98312 | tf_op jit(solution)/shard_map/ppermute | solution.py:284
  15.2 2.1 %transition_last.1 = bf16[64,32,64]{2,1,0:T(8,128)(2,1)} custom-call(bf16[64,32,64]{2,1,0:T(8,128)(2,1)S(1)} %get-tuple-element.35.x_ref, f32[1,64]{1,0:T(1,128)S(1)} %get-tuple-element.36.refs_0_, f32[1,64]{1,0:T(1,128)S(1)} %get-tuple-element.37.refs_1_, bf16[64,256]{1,0:T(8,128)(2,1)S(1)} %get-tuple-element.38.refs_2_, ...), custom_call_target="tpu_custom_call" | custom-call | flops 192000000 | bytes 960000 | tf_op jit(solution)/shard_map/transition_last/pallas_call | solution.py:311
  17.2 0.0 collective-permute-done.4.refs_1_
  17.2 0.4 %collective-permute-done.3.refs_0_ = f32[64,128]{1,0:T(8,128)S(1)} collective-permute-done((f32[64,128]{1,0:T(8,128)S(1)}, f32[64,128]{1,0:T(8,128)S(1)}, u32[]{:S(2)}, u32[]{:S(2)}) %collective-permute-start.3) | collective-permute-done | bytes 32800 | tf_op jit(solution)/shard_map/ppermute | solution.py:284
  17.6 0.8 %collective-permute-done.6.refs_2_ = f32[64,128]{1,0:T(8,128)S(1)} collective-permute-done((f32[64,128]{1,0:T(8,128)S(1)}, f32[64,128]{1,0:T(8,128)S(1)}, u32[]{:S(2)}, u32[]{:S(2)}) %collective-permute-start.6) | collective-permute-done | bytes 32800 | tf_op jit(solution)/shard_map/ppermute | solution.py:284
  18.4 0.7 %finish.1 = f32[64,128]{1,0:T(8,128)} custom-call(f32[64,128]{1,0:T(8,128)S(1)} %collective-permute-done.3.refs_0_, f32[64,128]{1,0:T(8,128)S(1)} %collective-permute-done.4.refs_1_, f32[64,128]{1,0:T(8,128)S(1)} %collective-permute-done.6.refs_2_, f32[64,128]{1,0:T(8,128)S(1)} %get-tuple-element.48.refs_3_, f32[1,128]{1,0:T(1,128)S(1)} %get-tuple-element.42.refs_4_), custom_call_target="tpu_custom_call" | custom-call | tf_op jit(solution)/shard_map/finish/pallas_call | solution.py:423
  (8 shorter events, 0.1 us)
Async XLA Ops:
  3.9 1.5 %collective-permute-start.1 = (f32[256,128]{1,0:T(8,128)S(1)}, f32[256,128]{1,0:T(8,128)S(1)}, u32[]{:S(2)}, u32[]{:S(2)}) collective-permute-start(f32[256,128]{1,0:T(8,128)S(1)} %get-tuple-element.29), channel_id=1, source_target_pairs={{0,1},{1,0},{2,3},{3,2},{4,5},{5,4},{6,7},{7,6},{8,9},{9,8},{10,11... | collective-permute-start | bytes 393224 | tf_op jit(solution)/shard_map/ppermute | solution.py:278
  4.4 3.7 %collective-permute-start = (f32[256,128]{1,0:T(8,128)S(1)}, f32[256,128]{1,0:T(8,128)S(1)}, u32[]{:S(2)}, u32[]{:S(2)}) collective-permute-start(f32[256,128]{1,0:T(8,128)S(1)} %get-tuple-element.28), channel_id=1, source_target_pairs={{0,1},{1,0},{2,3},{3,2},{4,5},{5,4},{6,7},{7,6},{8,9},{9,8},{10,11... | collective-permute-start | bytes 393224 | tf_op jit(solution)/shard_map/ppermute | solution.py:278
  5.5 4.9 %collective-permute-start.2 = (f32[2,64,128]{2,1,0:T(8,128)S(1)}, f32[2,64,128]{2,1,0:T(8,128)S(1)}, u32[]{:S(2)}, u32[]{:S(2)}) collective-permute-start(f32[2,64,128]{2,1,0:T(8,128)S(1)} %bitcast.25), channel_id=1, source_target_pairs={{0,3},{1,2},{2,1},{3,0},{4,7},{5,6},{6,5},{7,4},{8,11},{9,10},{10,... | collective-permute-start | bytes 196616 | tf_op jit(solution)/shard_map/ppermute | solution.py:278
  9.6 4.9 %collective-permute-start.5 = (f32[2,64,128]{2,1,0:T(8,128)S(1)}, f32[2,64,128]{2,1,0:T(8,128)S(1)}, u32[]{:S(2)}, u32[]{:S(2)}) collective-permute-start(f32[2,64,128]{2,1,0:T(8,128)S(1)} %bitcast.24), channel_id=1, source_target_pairs={{0,3},{1,2},{2,1},{3,0},{4,7},{5,6},{6,5},{7,4},{8,11},{9,10},{10,... | collective-permute-start | bytes 196616 | tf_op jit(solution)/shard_map/ppermute | solution.py:278
  10.4 6.9 %collective-permute-start.4 = (f32[64,128]{1,0:T(8,128)S(1)}, f32[64,128]{1,0:T(8,128)S(1)}, u32[]{:S(2)}, u32[]{:S(2)}) collective-permute-start(f32[64,128]{1,0:T(8,128)S(1)} %get-tuple-element.50), channel_id=1, source_target_pairs={{0,9},{1,8},{2,11},{3,10},{4,12},{5,13},{6,14},{7,15},{8,4},{9,5},... | collective-permute-start | bytes 98312 | tf_op jit(solution)/shard_map/ppermute | solution.py:284
  13.4 4.3 %collective-permute-start.3 = (f32[64,128]{1,0:T(8,128)S(1)}, f32[64,128]{1,0:T(8,128)S(1)}, u32[]{:S(2)}, u32[]{:S(2)}) collective-permute-start(f32[64,128]{1,0:T(8,128)S(1)} %get-tuple-element.51), channel_id=1, source_target_pairs={{0,13},{1,12},{2,15},{3,14},{4,8},{5,9},{6,10},{7,11},{8,1},{9,0},... | collective-permute-start | bytes 98312 | tf_op jit(solution)/shard_map/ppermute | solution.py:284
  14.5 3.9 %collective-permute-start.6 = (f32[64,128]{1,0:T(8,128)S(1)}, f32[64,128]{1,0:T(8,128)S(1)}, u32[]{:S(2)}, u32[]{:S(2)}) collective-permute-start(f32[64,128]{1,0:T(8,128)S(1)} %get-tuple-element.49), channel_id=1, source_target_pairs={{0,5},{1,4},{2,7},{3,6},{4,1},{5,0},{6,3},{7,2},{8,12},{9,13},{10,... | collective-permute-start | bytes 98312 | tf_op jit(solution)/shard_map/ppermute | solution.py:284

commit v6 on v5

--- a/solution.py
+++ b/solution.py
@@ -13,7 +13,7 @@
 LANES = 128
 VMEM_LIMIT = 48 * 1024 * 1024
 STEP = 16
-JOIN = 2
+JOIN = 4
 CHUNK = 256
 FIRST_HOP = (2, 3, 1, 0)
 SECOND_HOP = (3, 2, 0, 1)
@@ -117,7 +117,7 @@
 
 
 def outer_second_kernel(left_ref, right_ref, coupling_ref, counts_ref, here_ref, away_ref, x_mat):
-    outer_half(left_ref[...], right_ref[...], coupling_ref[...], counts_ref[...], x_mat, here_ref, away_ref)
+    outer_half(left_ref[...], right_ref, coupling_ref[...], counts_ref[...], x_mat, here_ref, away_ref)
 
 
 def outer_kernel(relative, n_inputs, n_handed, *refs):

time: 19.3 us -> 19.3 us (level)
  no operation moved by 1% of the time
where the time goes in v6:
time: 19.3 us; the launch traced here: 19.1 us
  starting transfers between devices  8.38 us (43%)
  Pallas kernels  8.26 us (43%)
  waiting for transfers between devices  1.69 us (9%)
  between operations  0.72 us (4%)
    ppermute x3, starting transfers between devices, hop(): return lax.ppermute(array, 'rows', pairs)  4.78 us
    ppermute x4, starting transfers between devices, swap(): return lax.ppermute(array, 'rows', [(i, i ^ apart) for i in range(size)])  3.6 us
    pallas_call x2, Pallas kernels, transition(): pl.pallas_call(functools.partial(transition_last, len(parts)) if last els...  3.46 us
    pallas_call x1, Pallas kernels, body(): pl.pallas_call(functools.partial(outer_kernel, relative, len(operands), l...  3.27 us
    ppermute x3, waiting for transfers between devices, hop(): return lax.ppermute(array, 'rows', pairs)  1.18 us
    pallas_call x1, Pallas kernels, body(): pl.pallas_call(outer_second_kernel, out_shape=[inside((pairs // 4, pair_c...  0.82 us
    pallas_call x1, Pallas kernels, body(): pl.pallas_call(functools.partial(finish_kernel, residues), out_shape=jax....  0.71 us
    ppermute x4, waiting for transfers between devices, swap(): return lax.ppermute(array, 'rows', [(i, i ^ apart) for i in range(size)])  0.51 us
  transfers between devices with their start and end apart: 7, of which 4 were waited for; matrix products, arithmetic and copies ran while one was open for 0% of the time, Pallas kernels for 22%

profile of v6, /device:TPU:0, one launch (start us, length us, event | category | flops | bytes accessed | tf_op | source)
XLA Modules:
  0.0 19.1 jit_solution(5408663561326345318)
XLA Ops:
  0.6 3.3 %outer_products.1 = (f32[256,128]{1,0:T(8,128)S(1)}, f32[256,128]{1,0:T(8,128)S(1)}, bf16[128,256]{1,0:T(8,128)(2,1)S(1)}, bf16[1024,256]{1,0:T(8,128)(2,1)S(1)}...) custom-call(bf16[64,32,64]{2,1,0:T(8,128)(2,1)} %refs_0_.1, ...), custom_call_target="tpu_custom_call" | custom-call | tf_op jit(solution)/shard_map/outer_products/pallas_call | solution.py:381
  3.9 0.5 %collective-permute-start.1 = (f32[256,128]{1,0:T(8,128)S(1)}, f32[256,128]{1,0:T(8,128)S(1)}, u32[]{:S(2)}, u32[]{:S(2)}) collective-permute-start(f32[256,128]{1,0:T(8,128)S(1)} %get-tuple-element.29), channel_id=1, source_target_pairs={{0,1},{1,0},{2,3},{3,2},{4,5},{5,4},{6,7},{7,6},{8,9},{9,8},{10,11... | collective-permute-start | bytes 393224 | tf_op jit(solution)/shard_map/ppermute | solution.py:278
  4.4 0.1 collective-permute-start
  4.5 0.8 %outer_second.1 = (f32[256,128]{1,0:T(8,128)S(1)}, f32[256,128]{1,0:T(8,128)S(1)}) custom-call(bf16[128,256]{1,0:T(8,128)(2,1)S(1)} %get-tuple-element.23.left_ref, bf16[1024,256]{1,0:T(8,128)(2,1)S(1)} %get-tuple-element.24.right_ref, bf16[1024,128]{1,0:T(8,128)(2,1)S(1)} %get-tuple-element.25.coupling_ref, f32[16,128]{1,0:T(8,128)S(1)} %get-tuple-element.26.counts_ref), custom_call_target="tpu_custom_call" | custom-call | flops 1000000000 | bytes 2000000 | tf_op jit(solution)/shard_map/outer_second/pallas_call | solution.py:397
  5.3 0.1 collective-permute-done.1
  5.5 2.7 %collective-permute-start.2 = (f32[2,64,128]{2,1,0:T(8,128)S(1)}, f32[2,64,128]{2,1,0:T(8,128)S(1)}, u32[]{:S(2)}, u32[]{:S(2)}) collective-permute-start(f32[2,64,128]{2,1,0:T(8,128)S(1)} %bitcast.25), channel_id=1, source_target_pairs={{0,3},{1,2},{2,1},{3,0},{4,7},{5,6},{6,5},{7,4},{8,11},{9,10},{10,... | collective-permute-start | bytes 196616 | tf_op jit(solution)/shard_map/ppermute | solution.py:278
  8.2 0.0 collective-permute-done
  8.2 1.4 %transition_part.1.refs_5_ = bf16[32,32,64]{2,1,0:T(8,128)(2,1)S(1)} custom-call(bf16[64,32,64]{2,1,0:T(8,128)(2,1)S(1)} %get-tuple-element.35.x_ref, f32[1,64]{1,0:T(1,128)S(1)} %get-tuple-element.36.refs_0_, f32[1,64]{1,0:T(1,128)S(1)} %get-tuple-element.37.refs_1_, bf16[64,256]{1,0:T(8,128)(2,1)S(1)} %get-tuple-element.38.refs_2_, ...), custom_call_target="tpu_custom_call" | custom-call | flops 192000000 | bytes 960000 | tf_op jit(solution)/shard_map/transition_part/pallas_call | solution.py:311
  9.6 0.3 %collective-permute-start.5 = (f32[2,64,128]{2,1,0:T(8,128)S(1)}, f32[2,64,128]{2,1,0:T(8,128)S(1)}, u32[]{:S(2)}, u32[]{:S(2)}) collective-permute-start(f32[2,64,128]{2,1,0:T(8,128)S(1)} %bitcast.24), channel_id=1, source_target_pairs={{0,3},{1,2},{2,1},{3,0},{4,7},{5,6},{6,5},{7,4},{8,11},{9,10},{10,... | collective-permute-start | bytes 196616 | tf_op jit(solution)/shard_map/ppermute | solution.py:278
  9.9 0.4 %collective-permute-done.2 = f32[2,64,128]{2,1,0:T(8,128)S(1)} collective-permute-done((f32[2,64,128]{2,1,0:T(8,128)S(1)}, f32[2,64,128]{2,1,0:T(8,128)S(1)}, u32[]{:S(2)}, u32[]{:S(2)}) %collective-permute-start.2) | collective-permute-done | bytes 65568 | tf_op jit(solution)/shard_map/ppermute | solution.py:278
  10.3 3.0 %collective-permute-start.4 = (f32[64,128]{1,0:T(8,128)S(1)}, f32[64,128]{1,0:T(8,128)S(1)}, u32[]{:S(2)}, u32[]{:S(2)}) collective-permute-start(f32[64,128]{1,0:T(8,128)S(1)} %get-tuple-element.50), channel_id=1, source_target_pairs={{0,9},{1,8},{2,11},{3,10},{4,12},{5,13},{6,14},{7,15},{8,4},{9,5},... | collective-permute-start | bytes 98312 | tf_op jit(solution)/shard_map/ppermute | solution.py:284
  13.4 1.1 %collective-permute-start.3 = (f32[64,128]{1,0:T(8,128)S(1)}, f32[64,128]{1,0:T(8,128)S(1)}, u32[]{:S(2)}, u32[]{:S(2)}) collective-permute-start(f32[64,128]{1,0:T(8,128)S(1)} %get-tuple-element.51), channel_id=1, source_target_pairs={{0,13},{1,12},{2,15},{3,14},{4,8},{5,9},{6,10},{7,11},{8,1},{9,0},... | collective-permute-start | bytes 98312 | tf_op jit(solution)/shard_map/ppermute | solution.py:284
  14.5 0.0 collective-permute-done.5
  14.5 0.7 %collective-permute-start.6 = (f32[64,128]{1,0:T(8,128)S(1)}, f32[64,128]{1,0:T(8,128)S(1)}, u32[]{:S(2)}, u32[]{:S(2)}) collective-permute-start(f32[64,128]{1,0:T(8,128)S(1)} %get-tuple-element.49), channel_id=1, source_target_pairs={{0,5},{1,4},{2,7},{3,6},{4,1},{5,0},{6,3},{7,2},{8,12},{9,13},{10,... | collective-permute-start | bytes 98312 | tf_op jit(solution)/shard_map/ppermute | solution.py:284
  15.2 2.1 %transition_last.1 = bf16[64,32,64]{2,1,0:T(8,128)(2,1)} custom-call(bf16[64,32,64]{2,1,0:T(8,128)(2,1)S(1)} %get-tuple-element.35.x_ref, f32[1,64]{1,0:T(1,128)S(1)} %get-tuple-element.36.refs_0_, f32[1,64]{1,0:T(1,128)S(1)} %get-tuple-element.37.refs_1_, bf16[64,256]{1,0:T(8,128)(2,1)S(1)} %get-tuple-element.38.refs_2_, ...), custom_call_target="tpu_custom_call" | custom-call | flops 192000000 | bytes 960000 | tf_op jit(solution)/shard_map/transition_last/pallas_call | solution.py:311
  17.2 0.0 collective-permute-done.4.refs_1_
  17.2 0.4 %collective-permute-done.3.refs_0_ = f32[64,128]{1,0:T(8,128)S(1)} collective-permute-done((f32[64,128]{1,0:T(8,128)S(1)}, f32[64,128]{1,0:T(8,128)S(1)}, u32[]{:S(2)}, u32[]{:S(2)}) %collective-permute-start.3) | collective-permute-done | bytes 32800 | tf_op jit(solution)/shard_map/ppermute | solution.py:284
  17.6 0.8 %collective-permute-done.6.refs_2_ = f32[64,128]{1,0:T(8,128)S(1)} collective-permute-done((f32[64,128]{1,0:T(8,128)S(1)}, f32[64,128]{1,0:T(8,128)S(1)}, u32[]{:S(2)}, u32[]{:S(2)}) %collective-permute-start.6) | collective-permute-done | bytes 32800 | tf_op jit(solution)/shard_map/ppermute | solution.py:284
  18.4 0.7 %finish.1 = f32[64,128]{1,0:T(8,128)} custom-call(f32[64,128]{1,0:T(8,128)S(1)} %collective-permute-done.3.refs_0_, f32[64,128]{1,0:T(8,128)S(1)} %collective-permute-done.4.refs_1_, f32[64,128]{1,0:T(8,128)S(1)} %collective-permute-done.6.refs_2_, f32[64,128]{1,0:T(8,128)S(1)} %get-tuple-element.48.refs_3_, f32[1,128]{1,0:T(1,128)S(1)} %get-tuple-element.42.refs_4_), custom_call_target="tpu_custom_call" | custom-call | tf_op jit(solution)/shard_map/finish/pallas_call | solution.py:423
  (8 shorter events, 0.1 us)
Async XLA Ops:
  3.9 1.5 %collective-permute-start.1 = (f32[256,128]{1,0:T(8,128)S(1)}, f32[256,128]{1,0:T(8,128)S(1)}, u32[]{:S(2)}, u32[]{:S(2)}) collective-permute-start(f32[256,128]{1,0:T(8,128)S(1)} %get-tuple-element.29), channel_id=1, source_target_pairs={{0,1},{1,0},{2,3},{3,2},{4,5},{5,4},{6,7},{7,6},{8,9},{9,8},{10,11... | collective-permute-start | bytes 393224 | tf_op jit(solution)/shard_map/ppermute | solution.py:278
  4.4 3.7 %collective-permute-start = (f32[256,128]{1,0:T(8,128)S(1)}, f32[256,128]{1,0:T(8,128)S(1)}, u32[]{:S(2)}, u32[]{:S(2)}) collective-permute-start(f32[256,128]{1,0:T(8,128)S(1)} %get-tuple-element.28), channel_id=1, source_target_pairs={{0,1},{1,0},{2,3},{3,2},{4,5},{5,4},{6,7},{7,6},{8,9},{9,8},{10,11... | collective-permute-start | bytes 393224 | tf_op jit(solution)/shard_map/ppermute | solution.py:278
  5.5 4.9 %collective-permute-start.2 = (f32[2,64,128]{2,1,0:T(8,128)S(1)}, f32[2,64,128]{2,1,0:T(8,128)S(1)}, u32[]{:S(2)}, u32[]{:S(2)}) collective-permute-start(f32[2,64,128]{2,1,0:T(8,128)S(1)} %bitcast.25), channel_id=1, source_target_pairs={{0,3},{1,2},{2,1},{3,0},{4,7},{5,6},{6,5},{7,4},{8,11},{9,10},{10,... | collective-permute-start | bytes 196616 | tf_op jit(solution)/shard_map/ppermute | solution.py:278
  9.6 4.9 %collective-permute-start.5 = (f32[2,64,128]{2,1,0:T(8,128)S(1)}, f32[2,64,128]{2,1,0:T(8,128)S(1)}, u32[]{:S(2)}, u32[]{:S(2)}) collective-permute-start(f32[2,64,128]{2,1,0:T(8,128)S(1)} %bitcast.24), channel_id=1, source_target_pairs={{0,3},{1,2},{2,1},{3,0},{4,7},{5,6},{6,5},{7,4},{8,11},{9,10},{10,... | collective-permute-start | bytes 196616 | tf_op jit(solution)/shard_map/ppermute | solution.py:278
  10.3 6.9 %collective-permute-start.4 = (f32[64,128]{1,0:T(8,128)S(1)}, f32[64,128]{1,0:T(8,128)S(1)}, u32[]{:S(2)}, u32[]{:S(2)}) collective-permute-start(f32[64,128]{1,0:T(8,128)S(1)} %get-tuple-element.50), channel_id=1, source_target_pairs={{0,9},{1,8},{2,11},{3,10},{4,12},{5,13},{6,14},{7,15},{8,4},{9,5},... | collective-permute-start | bytes 98312 | tf_op jit(solution)/shard_map/ppermute | solution.py:284
  13.4 4.3 %collective-permute-start.3 = (f32[64,128]{1,0:T(8,128)S(1)}, f32[64,128]{1,0:T(8,128)S(1)}, u32[]{:S(2)}, u32[]{:S(2)}) collective-permute-start(f32[64,128]{1,0:T(8,128)S(1)} %get-tuple-element.51), channel_id=1, source_target_pairs={{0,13},{1,12},{2,15},{3,14},{4,8},{5,9},{6,10},{7,11},{8,1},{9,0},... | collective-permute-start | bytes 98312 | tf_op jit(solution)/shard_map/ppermute | solution.py:284
  14.5 3.9 %collective-permute-start.6 = (f32[64,128]{1,0:T(8,128)S(1)}, f32[64,128]{1,0:T(8,128)S(1)}, u32[]{:S(2)}, u32[]{:S(2)}) collective-permute-start(f32[64,128]{1,0:T(8,128)S(1)} %get-tuple-element.49), channel_id=1, source_target_pairs={{0,5},{1,4},{2,7},{3,6},{4,1},{5,0},{6,3},{7,2},{8,12},{9,13},{10,... | collective-permute-start | bytes 98312 | tf_op jit(solution)/shard_map/ppermute | solution.py:284

commit v7 on v6

--- a/solution.py
+++ b/solution.py
@@ -167,6 +167,9 @@
     position = jnp.where(diagonal, position_ref[...].astype(F32), 0.0).sum(axis=1, keepdims=True)
     valid = (presence_ref[...].astype(F32) * position).astype(BF16)
     flags = dot(valid, spread, ((0,), (0,)))
+    counts = dot(dot(order, valid).astype(BF16), valid, ((1,), (1,)))
+    counts = jnp.concatenate([counts, jnp.zeros((residues, LANES - residues), F32)], axis=1)
+    counts_ref[...] = counts[:half]
     flags = jnp.concatenate(
         [flags[:, p * 2 * channels : (p + 1) * 2 * channels] for p in range(half)], axis=0
     )
@@ -201,9 +204,6 @@
     right = dot(normed, block_pair(repeated), ((1,), (1,))).astype(BF16)
     right_ref[...] = right
     left_ref[...] = left[: groups * half]
-    counts = dot(dot(order, valid).astype(BF16), valid, ((1,), (1,)))
-    counts = jnp.concatenate([counts, jnp.zeros((residues, LANES - residues), F32)], axis=1)
-    counts_ref[...] = counts[:half]
     outer_half(left[groups * half :], right, coupling_ref[...], counts[half:], x_mat, here_ref, away_ref)
     for copy in copies[early:]:
         copy.wait()

time: 19.3 us -> 19.3 us (level)
  no operation moved by 1% of the time
where the time goes in v7:
time: 19.3 us; the launch traced here: 19.1 us
  starting transfers between devices  8.37 us (43%)
  Pallas kernels  8.28 us (43%)
  waiting for transfers between devices  1.69 us (9%)
  between operations  0.72 us (4%)
    ppermute x3, starting transfers between devices, hop(): return lax.ppermute(array, 'rows', pairs)  4.77 us
    ppermute x4, starting transfers between devices, swap(): return lax.ppermute(array, 'rows', [(i, i ^ apart) for i in range(size)])  3.61 us
    pallas_call x2, Pallas kernels, transition(): pl.pallas_call(functools.partial(transition_last, len(parts)) if last els...  3.47 us
    pallas_call x1, Pallas kernels, body(): pl.pallas_call(functools.partial(outer_kernel, relative, len(operands), l...  3.28 us
    ppermute x3, waiting for transfers between devices, hop(): return lax.ppermute(array, 'rows', pairs)  1.18 us
    pallas_call x1, Pallas kernels, body(): pl.pallas_call(outer_second_kernel, out_shape=[inside((pairs // 4, pair_c...  0.82 us
    pallas_call x1, Pallas kernels, body(): pl.pallas_call(functools.partial(finish_kernel, residues), out_shape=jax....  0.71 us
    ppermute x4, waiting for transfers between devices, swap(): return lax.ppermute(array, 'rows', [(i, i ^ apart) for i in range(size)])  0.51 us
  transfers between devices with their start and end apart: 7, of which 4 were waited for; matrix products, arithmetic and copies ran while one was open for 0% of the time, Pallas kernels for 22%

profile of v7, /device:TPU:0, one launch (start us, length us, event | category | flops | bytes accessed | tf_op | source)
XLA Modules:
  0.0 19.1 jit_solution(13280750343765432547)
XLA Ops:
  0.6 3.3 %outer_products.1 = (f32[256,128]{1,0:T(8,128)S(1)}, f32[256,128]{1,0:T(8,128)S(1)}, bf16[128,256]{1,0:T(8,128)(2,1)S(1)}, bf16[1024,256]{1,0:T(8,128)(2,1)S(1)}...) custom-call(bf16[64,32,64]{2,1,0:T(8,128)(2,1)} %refs_0_.1, ...), custom_call_target="tpu_custom_call" | custom-call | tf_op jit(solution)/shard_map/outer_products/pallas_call | solution.py:381
  3.9 0.5 %collective-permute-start.1 = (f32[256,128]{1,0:T(8,128)S(1)}, f32[256,128]{1,0:T(8,128)S(1)}, u32[]{:S(2)}, u32[]{:S(2)}) collective-permute-start(f32[256,128]{1,0:T(8,128)S(1)} %get-tuple-element.29), channel_id=1, source_target_pairs={{0,1},{1,0},{2,3},{3,2},{4,5},{5,4},{6,7},{7,6},{8,9},{9,8},{10,11... | collective-permute-start | bytes 393224 | tf_op jit(solution)/shard_map/ppermute | solution.py:278
  4.4 0.1 collective-permute-start
  4.5 0.8 %outer_second.1 = (f32[256,128]{1,0:T(8,128)S(1)}, f32[256,128]{1,0:T(8,128)S(1)}) custom-call(bf16[128,256]{1,0:T(8,128)(2,1)S(1)} %get-tuple-element.23.left_ref, bf16[1024,256]{1,0:T(8,128)(2,1)S(1)} %get-tuple-element.24.right_ref, bf16[1024,128]{1,0:T(8,128)(2,1)S(1)} %get-tuple-element.25.coupling_ref, f32[16,128]{1,0:T(8,128)S(1)} %get-tuple-element.26.counts_ref), custom_call_target="tpu_custom_call" | custom-call | flops 1000000000 | bytes 2000000 | tf_op jit(solution)/shard_map/outer_second/pallas_call | solution.py:397
  5.3 0.1 collective-permute-done.1
  5.5 2.7 %collective-permute-start.2 = (f32[2,64,128]{2,1,0:T(8,128)S(1)}, f32[2,64,128]{2,1,0:T(8,128)S(1)}, u32[]{:S(2)}, u32[]{:S(2)}) collective-permute-start(f32[2,64,128]{2,1,0:T(8,128)S(1)} %bitcast.25), channel_id=1, source_target_pairs={{0,3},{1,2},{2,1},{3,0},{4,7},{5,6},{6,5},{7,4},{8,11},{9,10},{10,... | collective-permute-start | bytes 196616 | tf_op jit(solution)/shard_map/ppermute | solution.py:278
  8.2 0.0 collective-permute-done
  8.2 1.4 %transition_part.1.refs_5_ = bf16[32,32,64]{2,1,0:T(8,128)(2,1)S(1)} custom-call(bf16[64,32,64]{2,1,0:T(8,128)(2,1)S(1)} %get-tuple-element.35.x_ref, f32[1,64]{1,0:T(1,128)S(1)} %get-tuple-element.36.refs_0_, f32[1,64]{1,0:T(1,128)S(1)} %get-tuple-element.37.refs_1_, bf16[64,256]{1,0:T(8,128)(2,1)S(1)} %get-tuple-element.38.refs_2_, ...), custom_call_target="tpu_custom_call" | custom-call | flops 192000000 | bytes 960000 | tf_op jit(solution)/shard_map/transition_part/pallas_call | solution.py:311
  9.6 0.3 %collective-permute-start.5 = (f32[2,64,128]{2,1,0:T(8,128)S(1)}, f32[2,64,128]{2,1,0:T(8,128)S(1)}, u32[]{:S(2)}, u32[]{:S(2)}) collective-permute-start(f32[2,64,128]{2,1,0:T(8,128)S(1)} %bitcast.24), channel_id=1, source_target_pairs={{0,3},{1,2},{2,1},{3,0},{4,7},{5,6},{6,5},{7,4},{8,11},{9,10},{10,... | collective-permute-start | bytes 196616 | tf_op jit(solution)/shard_map/ppermute | solution.py:278
  9.9 0.4 %collective-permute-done.2 = f32[2,64,128]{2,1,0:T(8,128)S(1)} collective-permute-done((f32[2,64,128]{2,1,0:T(8,128)S(1)}, f32[2,64,128]{2,1,0:T(8,128)S(1)}, u32[]{:S(2)}, u32[]{:S(2)}) %collective-permute-start.2) | collective-permute-done | bytes 65568 | tf_op jit(solution)/shard_map/ppermute | solution.py:278
  10.4 3.0 %collective-permute-start.4 = (f32[64,128]{1,0:T(8,128)S(1)}, f32[64,128]{1,0:T(8,128)S(1)}, u32[]{:S(2)}, u32[]{:S(2)}) collective-permute-start(f32[64,128]{1,0:T(8,128)S(1)} %get-tuple-element.50), channel_id=1, source_target_pairs={{0,9},{1,8},{2,11},{3,10},{4,12},{5,13},{6,14},{7,15},{8,4},{9,5},... | collective-permute-start | bytes 98312 | tf_op jit(solution)/shard_map/ppermute | solution.py:284
  13.4 1.1 %collective-permute-start.3 = (f32[64,128]{1,0:T(8,128)S(1)}, f32[64,128]{1,0:T(8,128)S(1)}, u32[]{:S(2)}, u32[]{:S(2)}) collective-permute-start(f32[64,128]{1,0:T(8,128)S(1)} %get-tuple-element.51), channel_id=1, source_target_pairs={{0,13},{1,12},{2,15},{3,14},{4,8},{5,9},{6,10},{7,11},{8,1},{9,0},... | collective-permute-start | bytes 98312 | tf_op jit(solution)/shard_map/ppermute | solution.py:284
  14.5 0.0 collective-permute-done.5
  14.5 0.7 %collective-permute-start.6 = (f32[64,128]{1,0:T(8,128)S(1)}, f32[64,128]{1,0:T(8,128)S(1)}, u32[]{:S(2)}, u32[]{:S(2)}) collective-permute-start(f32[64,128]{1,0:T(8,128)S(1)} %get-tuple-element.49), channel_id=1, source_target_pairs={{0,5},{1,4},{2,7},{3,6},{4,1},{5,0},{6,3},{7,2},{8,12},{9,13},{10,... | collective-permute-start | bytes 98312 | tf_op jit(solution)/shard_map/ppermute | solution.py:284
  15.2 2.1 %transition_last.1 = bf16[64,32,64]{2,1,0:T(8,128)(2,1)} custom-call(bf16[64,32,64]{2,1,0:T(8,128)(2,1)S(1)} %get-tuple-element.35.x_ref, f32[1,64]{1,0:T(1,128)S(1)} %get-tuple-element.36.refs_0_, f32[1,64]{1,0:T(1,128)S(1)} %get-tuple-element.37.refs_1_, bf16[64,256]{1,0:T(8,128)(2,1)S(1)} %get-tuple-element.38.refs_2_, ...), custom_call_target="tpu_custom_call" | custom-call | flops 192000000 | bytes 960000 | tf_op jit(solution)/shard_map/transition_last/pallas_call | solution.py:311
  17.2 0.0 collective-permute-done.4.refs_1_
  17.3 0.4 %collective-permute-done.3.refs_0_ = f32[64,128]{1,0:T(8,128)S(1)} collective-permute-done((f32[64,128]{1,0:T(8,128)S(1)}, f32[64,128]{1,0:T(8,128)S(1)}, u32[]{:S(2)}, u32[]{:S(2)}) %collective-permute-start.3) | collective-permute-done | bytes 32800 | tf_op jit(solution)/shard_map/ppermute | solution.py:284
  17.6 0.8 %collective-permute-done.6.refs_2_ = f32[64,128]{1,0:T(8,128)S(1)} collective-permute-done((f32[64,128]{1,0:T(8,128)S(1)}, f32[64,128]{1,0:T(8,128)S(1)}, u32[]{:S(2)}, u32[]{:S(2)}) %collective-permute-start.6) | collective-permute-done | bytes 32800 | tf_op jit(solution)/shard_map/ppermute | solution.py:284
  18.4 0.7 %finish.1 = f32[64,128]{1,0:T(8,128)} custom-call(f32[64,128]{1,0:T(8,128)S(1)} %collective-permute-done.3.refs_0_, f32[64,128]{1,0:T(8,128)S(1)} %collective-permute-done.4.refs_1_, f32[64,128]{1,0:T(8,128)S(1)} %collective-permute-done.6.refs_2_, f32[64,128]{1,0:T(8,128)S(1)} %get-tuple-element.48.refs_3_, f32[1,128]{1,0:T(1,128)S(1)} %get-tuple-element.42.refs_4_), custom_call_target="tpu_custom_call" | custom-call | tf_op jit(solution)/shard_map/finish/pallas_call | solution.py:423
  (8 shorter events, 0.1 us)
Async XLA Ops:
  3.9 1.5 %collective-permute-start.1 = (f32[256,128]{1,0:T(8,128)S(1)}, f32[256,128]{1,0:T(8,128)S(1)}, u32[]{:S(2)}, u32[]{:S(2)}) collective-permute-start(f32[256,128]{1,0:T(8,128)S(1)} %get-tuple-element.29), channel_id=1, source_target_pairs={{0,1},{1,0},{2,3},{3,2},{4,5},{5,4},{6,7},{7,6},{8,9},{9,8},{10,11... | collective-permute-start | bytes 393224 | tf_op jit(solution)/shard_map/ppermute | solution.py:278
  4.4 3.7 %collective-permute-start = (f32[256,128]{1,0:T(8,128)S(1)}, f32[256,128]{1,0:T(8,128)S(1)}, u32[]{:S(2)}, u32[]{:S(2)}) collective-permute-start(f32[256,128]{1,0:T(8,128)S(1)} %get-tuple-element.28), channel_id=1, source_target_pairs={{0,1},{1,0},{2,3},{3,2},{4,5},{5,4},{6,7},{7,6},{8,9},{9,8},{10,11... | collective-permute-start | bytes 393224 | tf_op jit(solution)/shard_map/ppermute | solution.py:278
  5.5 4.9 %collective-permute-start.2 = (f32[2,64,128]{2,1,0:T(8,128)S(1)}, f32[2,64,128]{2,1,0:T(8,128)S(1)}, u32[]{:S(2)}, u32[]{:S(2)}) collective-permute-start(f32[2,64,128]{2,1,0:T(8,128)S(1)} %bitcast.25), channel_id=1, source_target_pairs={{0,3},{1,2},{2,1},{3,0},{4,7},{5,6},{6,5},{7,4},{8,11},{9,10},{10,... | collective-permute-start | bytes 196616 | tf_op jit(solution)/shard_map/ppermute | solution.py:278
  9.6 4.9 %collective-permute-start.5 = (f32[2,64,128]{2,1,0:T(8,128)S(1)}, f32[2,64,128]{2,1,0:T(8,128)S(1)}, u32[]{:S(2)}, u32[]{:S(2)}) collective-permute-start(f32[2,64,128]{2,1,0:T(8,128)S(1)} %bitcast.24), channel_id=1, source_target_pairs={{0,3},{1,2},{2,1},{3,0},{4,7},{5,6},{6,5},{7,4},{8,11},{9,10},{10,... | collective-permute-start | bytes 196616 | tf_op jit(solution)/shard_map/ppermute | solution.py:278
  10.4 6.9 %collective-permute-start.4 = (f32[64,128]{1,0:T(8,128)S(1)}, f32[64,128]{1,0:T(8,128)S(1)}, u32[]{:S(2)}, u32[]{:S(2)}) collective-permute-start(f32[64,128]{1,0:T(8,128)S(1)} %get-tuple-element.50), channel_id=1, source_target_pairs={{0,9},{1,8},{2,11},{3,10},{4,12},{5,13},{6,14},{7,15},{8,4},{9,5},... | collective-permute-start | bytes 98312 | tf_op jit(solution)/shard_map/ppermute | solution.py:284
  13.4 4.3 %collective-permute-start.3 = (f32[64,128]{1,0:T(8,128)S(1)}, f32[64,128]{1,0:T(8,128)S(1)}, u32[]{:S(2)}, u32[]{:S(2)}) collective-permute-start(f32[64,128]{1,0:T(8,128)S(1)} %get-tuple-element.51), channel_id=1, source_target_pairs={{0,13},{1,12},{2,15},{3,14},{4,8},{5,9},{6,10},{7,11},{8,1},{9,0},... | collective-permute-start | bytes 98312 | tf_op jit(solution)/shard_map/ppermute | solution.py:284
  14.5 3.9 %collective-permute-start.6 = (f32[64,128]{1,0:T(8,128)S(1)}, f32[64,128]{1,0:T(8,128)S(1)}, u32[]{:S(2)}, u32[]{:S(2)}) collective-permute-start(f32[64,128]{1,0:T(8,128)S(1)} %get-tuple-element.49), channel_id=1, source_target_pairs={{0,5},{1,4},{2,7},{3,6},{4,1},{5,0},{6,3},{7,2},{8,12},{9,13},{10,... | collective-permute-start | bytes 98312 | tf_op jit(solution)/shard_map/ppermute | solution.py:284
